TPU v7x, 128 devices: a whole 4x4x4 slice. The times are simulated.
128 devices in a mesh: row: 16 (over y_hi, z, core), col: 4 (over x), gz: 2 (over y_lo).
Axes of the slice: x: 4, y: 4 (y_hi: 2, y_lo: 2; y = y_hi * 2 + y_lo), z: 4, core: 2. Of those that a mesh axis runs over, the one named last changes fastest.
Arguments:
- velocity_hat: bfloat16 [3, 2, 2, 4096, 4096], P(None, None, 'gz', ('row', 'col')), may hold values from -6 to 6
Outputs:
- smoothed: float32 [2, 4096, 4096], P('gz', 'col', 'row')
All inputs are finite; a program needn't handle non-finite values.
Results may differ from a plain program's by a relative error of at most 0.002.
Values may be sent and summed in bfloat16 or wider, within the bound.
No kernel may reach another device: no remote copies, remote signals or barrier semaphores. Data moves between devices by JAX's collectives and lax.ppermute only.
A program may use at most 128 MiB of HBM per device.

v0:
```python
import math

import jax
import jax.numpy as jnp
import numpy as np
from jax import lax
from jax.experimental import pallas as pl
from jax.experimental.pallas import tpu as pltpu
from jax.sharding import PartitionSpec as P

GRID = 4096
RELAX = 0.15
VMEM_LIMIT = 48 * 1024 * 1024
NT = (((1,), (1,)), ((), ()))


def split_bf16(table):
    high = table.astype(jnp.bfloat16)
    low = (table - high.astype(np.float64)).astype(jnp.bfloat16)
    return np.concatenate([high, low], axis=0)


def tables():
    k = np.arange(128)
    blocks = []
    for s in range(2):
        angle = 2 * np.pi * ((np.arange(64)[:, None] * 2 + s) * k[None, :] % 128) / 128
        c, d = np.cos(angle), np.sin(angle)
        blocks.append(np.concatenate([c, -d], axis=1))
        blocks.append(np.concatenate([d, c], axis=1))
    x_matrix = split_bf16(np.concatenate(blocks, axis=0))
    angle = 2 * np.pi * (np.arange(32)[:, None] * k[None, :]) / 4096
    x_twist = np.stack([np.cos(angle), np.sin(angle)]).astype(np.float32) / 64
    j = np.arange(64)
    angle = 2 * np.pi * (j[:, None] * j[None, :] % 64) / 64
    zero = np.zeros((64, 64))
    c, d = np.cos(angle), -np.sin(angle)
    y_matrix = split_bf16(
        np.concatenate(
            [np.concatenate([c, zero, d, zero], axis=1), np.concatenate([zero, c, zero, d], axis=1)], axis=0
        )
    )
    angle = 2 * np.pi * (j[:, None] * j[None, :]) / 4096
    y_twist = np.stack([np.cos(angle), np.sin(angle)]).astype(np.float32) / 64
    y_twist = np.concatenate([y_twist, y_twist], axis=2)
    return x_matrix, x_twist, y_matrix, y_twist


def turned(value, num, den):
    re, im = value
    num = num % den
    if num == 0:
        return value
    if 2 * num == den:
        return (-re, -im)
    if 4 * num == den:
        return (-im, re)
    if 4 * num == 3 * den:
        return (im, -re)
    if 8 * num == den:
        r = math.sqrt(0.5)
        return ((re - im) * r, (re + im) * r)
    if 8 * num == 3 * den:
        r = math.sqrt(0.5)
        return ((re + im) * -r, (re - im) * r)
    c, s = math.cos(2 * math.pi * num / den), math.sin(2 * math.pi * num / den)
    return (re * c - im * s, re * s + im * c)


def plus(a, b):
    return (a[0] + b[0], a[1] + b[1])


def minus(a, b):
    return (a[0] - b[0], a[1] - b[1])


def dft4(v):
    a, b = plus(v[0], v[2]), minus(v[0], v[2])
    c, d = plus(v[1], v[3]), minus(v[1], v[3])
    return [plus(a, c), (b[0] - d[1], b[1] + d[0]), minus(a, c), (b[0] + d[1], b[1] - d[0])]


def dft8(v):
    even, odd = dft4(v[0::2]), dft4(v[1::2])
    odd = [turned(odd[t], t, 8) for t in range(4)]
    return [plus(e, o) for e, o in zip(even, odd)] + [minus(e, o) for e, o in zip(even, odd)]


def x_kernel(fields, rows_local, *refs):
    n_in = 2 if fields == ("curl_z",) or fields[0] == "u" else 3
    n_out = 2 if len(fields) == 2 else 1
    ins, (matrix, twist), refs = refs[:n_in], refs[n_in : n_in + 2], refs[n_in + 2 :]
    outs, (stage, lines, spread) = refs[-3 - n_out : -3], refs[-3:]
    step = pl.program_id(0)
    scale = 2.0 * math.pi / GRID
    lane = lax.broadcasted_iota(jnp.int32, (16, 128), 1)
    row = lax.broadcasted_iota(jnp.int32, (16, 128), 0)
    start = lax.axis_index(("yh", "zc", "col")) * rows_local + step * 16
    ky = row + start
    wave_y = jnp.where(ky >= GRID // 2, ky - GRID, ky).astype(jnp.float32) * scale

    def tile(ref, part, q):
        return ref[0, part, :, pl.ds(q * 128, 128)].astype(jnp.float32)

    def wave_x(q):
        base = q * 128 - (GRID if q >= 16 else 0)
        return (lane + base).astype(jnp.float32) * scale

    def value_of(field, q):
        if field == "curl_z":
            u, v = ins
            wx = wave_x(q)
            return (
                wave_y * tile(u, 1, q) - wx * tile(v, 1, q),
                wx * tile(v, 0, q) - wave_y * tile(u, 0, q),
            )
        if field == "u":
            return (tile(ins[0], 0, q), tile(ins[0], 1, q))
        if field == "v":
            return (tile(ins[1], 0, q), tile(ins[1], 1, q))
        u, v, w = ins
        if field == "curl_x":
            return (tile(v, 0, q) - wave_y * tile(w, 1, q), tile(v, 1, q) + wave_y * tile(w, 0, q))
        wx = wave_x(q)
        return (wx * tile(w, 1, q) - tile(u, 0, q), -wx * tile(w, 0, q) - tile(u, 1, q))

    for index, field in enumerate(fields):
        for a in range(8):
            for b, value in enumerate(dft4([value_of(field, a + 8 * t) for t in range(4)])):
                value = turned(value, a * b, 32)
                stage[0, b * 8 + a] = value[0]
                stage[1, b * 8 + a] = value[1]
        for b in range(4):
            for t, value in enumerate(dft8([(stage[0, b * 8 + a], stage[1, b * 8 + a]) for a in range(8)])):
                n = b + 4 * t
                c, s = twist[0, n : n + 1, :], twist[1, n : n + 1, :]
                at = pl.ds(((n % 16) * 2 + n // 16) * 64 + step * 16, 16)
                lines[index, at, 0:128] = (value[0] * c - value[1] * s).astype(jnp.bfloat16)
                lines[index, at, 128:256] = (value[0] * s + value[1] * c).astype(jnp.bfloat16)

    @pl.when(step == 3)
    def _():
        for index in range(len(fields)):
            for pair in range(8):
                got = lax.dot_general(
                    matrix[...], lines[index, pl.ds(pair * 256, 256), :], NT, preferred_element_type=jnp.float32
                )
                got = got[0:256] + got[256:512]
                for half in range(2):
                    n16 = pair * 2 + half
                    for s in range(2):
                        for c in range(2):
                            at = (s * 2 + c) * 64
                            spread[pl.ds(c * 32 + s * 16 + n16, 64, stride=64), :] = got[
                                at : at + 64, half * 128 : half * 128 + 128
                            ]
            for half in range(2):
                first = (lax.axis_index("yh") + half) % 2 * 2048
                for b in range(32):
                    at = pl.ds(pl.multiple_of(first + b * 64, 64), 64)
                    block = spread[at, :].astype(jnp.bfloat16)
                    if n_out == 1:
                        outs[0][b, half * 64 : half * 64 + 64, :] = block
                    else:
                        outs[half][b, index * 64 : index * 64 + 64, :] = block


def x_transform(fields, parts, x_matrix, x_twist, after=()):
    rows_local = parts.shape[2]
    comps = (0, 1, 2) if fields[0] == "curl_x" else (0, 1)
    specs = [pl.BlockSpec((1, 2, 16, GRID), lambda i, comp=comp: (comp, 0, i, 0)) for comp in comps] + [
        pl.BlockSpec((512, 256), lambda i: (0, 0)),
        pl.BlockSpec((2, 32, 128), lambda i: (0, 0, 0)),
    ]
    specs += [pl.BlockSpec(memory_space=pl.ANY)] * len(after)
    return pl.pallas_call(
        lambda *refs: x_kernel(fields, rows_local, *refs),
        grid=(rows_local // 16,),
        in_specs=specs,
        out_specs=[pl.BlockSpec((32, 128, 128), lambda i: (0, 0, 0))] * len(fields),
        out_shape=[jax.ShapeDtypeStruct((32, 128, 128), jnp.bfloat16)] * len(fields),
        scratch_shapes=[
            pltpu.VMEM((2, 32, 16, 128), jnp.float32),
            pltpu.VMEM((len(fields), 2048, 256), jnp.bfloat16),
            pltpu.VMEM((4096, 128), jnp.float32),
        ],
        compiler_params=pltpu.CompilerParams(vmem_limit_bytes=VMEM_LIMIT),
        cost_estimate=pl.CostEstimate(flops=2**30, bytes_accessed=2**22, transcendentals=0),
        name="lines_" + "_".join(fields),
    )(*[parts] * len(comps), x_matrix, x_twist, *after)


def meet_kernel(own, came, near, across, out):
    for b in range(out.shape[0]):
        for index, sign in ((0, -1.0), (1, 1.0)):
            rows, term_rows = slice(index * 64, index * 64 + 64), slice(64 - index * 64, 128 - index * 64)
            for half, (field, term) in enumerate(((own, near), (came, across))):
                value = field[b, rows, :].astype(jnp.float32) + sign * term[b, term_rows, :].astype(jnp.float32)
                at = index * 128 + half * 64
                out[b, at : at + 64, :] = value.astype(jnp.bfloat16)


def meet(own, came, near, across):
    return pl.pallas_call(
        meet_kernel,
        grid=(4,),
        in_specs=[pl.BlockSpec((8, 128, 128), lambda i: (i, 0, 0))] * 4,
        out_specs=pl.BlockSpec((8, 256, 128), lambda i: (i, 0, 0)),
        out_shape=jax.ShapeDtypeStruct((32, 256, 128), jnp.bfloat16),
        compiler_params=pltpu.CompilerParams(vmem_limit_bytes=VMEM_LIMIT),
        cost_estimate=pl.CostEstimate(flops=2**20, bytes_accessed=2**22, transcendentals=0),
        name="meet",
    )(own, came, near, across)


def y_lines(sources, twist, stage, lines):
    def one(part, carry):
        def load(c, d):
            source, first = sources[d // 32]
            return source[d % 32, pl.ds(first + c * 32 + part * 16, 16), :].astype(jnp.float32)

        for a in range(8):
            values = [(load(0, a + 8 * t), load(1, a + 8 * t)) for t in range(8)]
            for b, value in enumerate(dft8(values)):
                value = turned(value, a * b, 64)
                stage[0, b * 8 + a] = value[0]
                stage[1, b * 8 + a] = value[1]
        for b in range(8):
            for t, value in enumerate(dft8([(stage[0, b * 8 + a], stage[1, b * 8 + a]) for a in range(8)])):
                n = b + 8 * t
                c, s = twist[0, n : n + 1, :], twist[1, n : n + 1, :]
                at = pl.ds(n * 32 + part * 16, 16)
                lines[at, 0:128] = (value[0] * c - value[1] * s).astype(jnp.bfloat16)
                lines[at, 128:256] = (value[0] * s + value[1] * c).astype(jnp.bfloat16)
        return carry

    lax.fori_loop(0, 2, one, 0)


def y_squares(sources, matrix, twist, stage, lines, add):
    y_lines(sources, twist, stage, lines)
    for chunk in range(8):
        got = lax.dot_general(
            matrix[...], lines[pl.ds(chunk * 256, 256), :], NT, preferred_element_type=jnp.float32
        )
        got = got[0:128] + got[128:256]
        add((slice(None), slice(chunk * 256, chunk * 256 + 256)), got * got)


def y_first(own, came, matrix, twist, out, stage, lines):
    def add(at, square):
        out[at] = 1.0 + square

    y_squares(((own, 0), (came, 0)), matrix, twist, stage, lines, add)


def y_next(source, before, matrix, twist, out, stage, lines):
    def add(at, square):
        out[at] = before[at] + square

    y_squares(((source, 0), (source, 64)), matrix, twist, stage, lines, add)


def y_last(source, before, matrix, twist, out, stage, lines, total):
    def add(at, square):
        total[at] = jnp.sqrt(before[at] + square)

    y_squares(((source, 128), (source, 192)), matrix, twist, stage, lines, add)

    def put(h, tile, value):
        value = value.astype(jnp.bfloat16)
        for c in range(4):
            for z in range(2):
                out[z * 4 + c, h * 16 : h * 16 + 16, tile * 128 : tile * 128 + 128] = value[c * 16 : c * 16 + 16]

    for h in range(2):
        rows = slice(h * 64, h * 64 + 64)
        for tile in range(16):
            put(h, tile + 1, total[rows, tile * 128 : tile * 128 + 128])
        put(h, 0, pltpu.roll(total[rows, 15 * 128 : 16 * 128], 1, 0))
        put(h, 17, pltpu.roll(total[rows, 0:128], 63, 0))


def y_transform(kernel, sources, y_matrix, y_twist):
    last = kernel is y_last
    sums = jax.ShapeDtypeStruct((128, 2048), jnp.float32)
    scratch = [pltpu.VMEM((2, 64, 16, 128), jnp.float32), pltpu.VMEM((2048, 256), jnp.bfloat16)]
    return pl.pallas_call(
        kernel,
        out_shape=jax.ShapeDtypeStruct((8, 32, 2304), jnp.bfloat16) if last else sums,
        scratch_shapes=scratch + ([pltpu.VMEM((128, 2048), jnp.float32)] if last else []),
        compiler_params=pltpu.CompilerParams(vmem_limit_bytes=VMEM_LIMIT),
        cost_estimate=pl.CostEstimate(flops=2**28, bytes_accessed=2**22, transcendentals=0),
        name=kernel.__name__,
    )(*sources, y_matrix, y_twist)


def smooth_coefficients():
    w = RELAX
    even = np.polynomial.polynomial.polypow([1 - 6 * w + 2 * w, w], 3)
    odd = np.polynomial.polynomial.polypow([1 - 6 * w - 2 * w, w], 3)
    return (even + odd) / 2, (even - odd) / 2


def regroup_kernel(field, own, other):
    me = lax.axis_index("gz")
    lane = lax.broadcasted_iota(jnp.int32, (16, 128), 1)

    def swapped(a, b, width):
        upper = (lane & width) != 0
        return (
            jnp.where(upper, pltpu.roll(b, width, 1), a),
            jnp.where(upper, b, pltpu.roll(a, 128 - width, 1)),
        )

    def regroup(z, target, tile):
        at = pl.ds(pl.multiple_of(tile * 128, 128), 128)
        for ch in range(2):
            v = {
                (c, h): field[z * 4 + ch * 2 + c, h * 16 : h * 16 + 16, at].astype(jnp.float32)
                for c in range(2)
                for h in range(2)
            }
            p = {}
            for h in range(2):
                p[0, h], p[1, h] = swapped(v[0, h], v[1, h], 64)
            for y1 in range(2):
                s0, s1 = swapped(p[y1, 0], p[y1, 1], 16)
                y00, y01 = swapped(s0, s1, 32)
                target[tile * 4 + y1 * 2, :, ch * 128 : ch * 128 + 128] = y00
                target[tile * 4 + y1 * 2 + 1, :, ch * 128 : ch * 128 + 128] = y01

    def both(step, carry):
        for t in range(3):
            regroup(me, own, step * 3 + t)
            regroup(1 - me, other, step * 3 + t)
        return carry

    lax.fori_loop(0, 6, both, 0)


def regroup(field):
    return pl.pallas_call(
        regroup_kernel,
        out_shape=[jax.ShapeDtypeStruct((72, 16, 256), jnp.float32)] * 2,
        compiler_params=pltpu.CompilerParams(vmem_limit_bytes=VMEM_LIMIT),
        cost_estimate=pl.CostEstimate(flops=2**24, bytes_accessed=2**23, transcendentals=0),
        name="regroup",
    )(field)


def edge_kernel(field, low, high):
    lane = lax.broadcasted_iota(jnp.int32, (16, 128), 1)
    for z in range(2):
        for group in range(5):
            last = first = jnp.zeros((16, 128), jnp.float32)
            for t in range(min(4, 18 - group * 4)):
                at = slice((group * 4 + t) * 128, (group * 4 + t) * 128 + 128)
                here = (lane & 24) == 8 * t
                last = jnp.where(here, pltpu.roll(field[z * 4 + 3, 16:32, at].astype(jnp.float32), 100 + 8 * t, 1), last)
                first = jnp.where(here, pltpu.roll(field[z * 4, 0:16, at].astype(jnp.float32), 4 + 8 * t, 1), first)
            low[z, :, group * 128 : group * 128 + 128] = last.astype(jnp.bfloat16)
            high[z, :, group * 128 : group * 128 + 128] = first.astype(jnp.bfloat16)


def edges(field):
    return pl.pallas_call(
        edge_kernel,
        out_shape=[jax.ShapeDtypeStruct((2, 16, 640), jnp.bfloat16)] * 2,
        compiler_params=pltpu.CompilerParams(vmem_limit_bytes=VMEM_LIMIT),
        name="edges",
    )(field)


def smooth_kernel(own, other, low, high, out, own_edge, other_edge, work, spread):
    own_c, other_c = [[float(v) for v in part] for part in smooth_coefficients()]
    me = lax.axis_index("gz")
    lane = lax.broadcasted_iota(jnp.int32, (16, 128), 1)
    is_low = (lane & 7) < 4

    def spread_edges(group, tiles):
        at = pl.ds(pl.multiple_of(group * 128, 128), 128)
        for z, target in ((me, own_edge), (1 - me, other_edge)):
            both = jnp.where(is_low, low[z, :, at].astype(jnp.float32), high[z, :, at].astype(jnp.float32))
            for t in range(tiles):
                for y in range(4):
                    target[(group * 4 + t) * 4 + y] = pltpu.roll(both, 124 - 32 * y - 8 * t, 1)

    def edge_group(group, carry):
        spread_edges(group, 4)
        return carry

    lax.fori_loop(0, 4, edge_group, 0)
    spread_edges(4, 2)

    def beside(ref, y, center):
        sides = pltpu.roll(center, 1, 1) + pltpu.roll(center, 383, 1)
        return sides + (ref(y - 1) + ref(y + 1))

    def own_at(y):
        return jnp.concatenate([own[y], own_edge[y]], axis=1)

    def other_at(y):
        return jnp.concatenate([other[y], other_edge[y]], axis=1)

    def each(begin, end, unroll, body):
        def some(step, carry):
            for t in range(unroll):
                body(begin + step * unroll + t)
            return carry

        lax.fori_loop(0, (end - begin) // unroll, some, 0)

    def first(y):
        center = own_at(y)
        work[0, y] = center * own_c[2] + other_at(y) * other_c[2] + beside(own_at, y, center) * own_c[3]

    def second(y):
        center = work[0, y]
        work[1, y] = own_at(y) * own_c[1] + other_at(y) * other_c[1] + beside(lambda i: work[0, i], y, center)

    def third(y):
        center = work[1, y]
        value = beside(lambda i: work[1, i], y, center)[:, 0:256]
        value = own[y] * own_c[0] + other[y] * other_c[0] + value
        for half in range(2):
            spread[pl.ds(half * 1024 + y - 4, 16, stride=64), :] = value[:, half * 128 : half * 128 + 128]

    each(2, 70, 4, first)
    each(3, 69, 6, second)
    each(4, 68, 4, third)
    for half in range(2):
        out[0, :, half * 128 : half * 128 + 128] = spread[pl.ds(half * 1024, 1024), :]


def smooth(own, other, low, high):
    return pl.pallas_call(
        smooth_kernel,
        out_shape=jax.ShapeDtypeStruct((1, 1024, 256), jnp.float32),
        scratch_shapes=[
            pltpu.VMEM((72, 16, 128), jnp.float32),
            pltpu.VMEM((72, 16, 128), jnp.float32),
            pltpu.VMEM((2, 72, 16, 384), jnp.float32),
            pltpu.VMEM((2048, 128), jnp.float32),
        ],
        compiler_params=pltpu.CompilerParams(vmem_limit_bytes=VMEM_LIMIT),
        name="smooth",
    )(own, other, low, high)


def ring(value, axis, steps):
    count = lax.axis_size(axis)
    return lax.ppermute(value, axis, [(i, (i + steps) % count) for i in range(count)])


def between_y(value, target):
    pairs = []
    for y_hi in range(2):
        for gz in range(2):
            to_hi, to_gz = target(y_hi, gz)
            pairs.append((y_hi * 2 + gz, to_hi * 2 + to_gz))
    return lax.ppermute(value, ("yh", "gz"), pairs)


def shards(velocity_hat):
    x_matrix, x_twist, y_matrix, y_twist = (jnp.asarray(t) for t in tables())
    parts = velocity_hat.reshape((3, 2) + velocity_hat.shape[3:])

    def exchanged(array, axes):
        return lax.all_to_all(array, axes, split_axis=0, concat_axis=0, tiled=True)

    def lines(fields, after=()):
        return x_transform(fields, parts, x_matrix, x_twist, after)

    curl_own, curl_other = lines(("curl_x", "curl_y"))
    curl_z = lines(("curl_z",), (curl_own,))[0]
    term_own, term_other = lines(("u", "v"), (curl_z,))
    came = between_y(curl_other, lambda y_hi, gz: (1 - y_hi, gz))
    near = between_y(term_own, lambda y_hi, gz: (y_hi, 1 - gz))
    across = between_y(term_other, lambda y_hi, gz: (1 - y_hi, 1 - gz))
    line_2 = exchanged(curl_z, ("zc", "col"))
    came_2 = between_y(line_2[:, 64:], lambda y_hi, gz: (1 - y_hi, gz))
    both = exchanged(meet(curl_own, came, near, across), ("zc", "col"))
    squares = y_transform(y_first, (line_2, came_2), y_matrix, y_twist)
    squares = y_transform(y_next, (both, squares), y_matrix, y_twist)
    magnitude = y_transform(y_last, (both, squares), y_matrix, y_twist)
    field = exchanged(magnitude, ("gz", "col"))
    last, first = edges(field)
    low, high = ring(last, ("yh", "zc"), 1), ring(first, ("yh", "zc"), -1)
    own, other = regroup(field)
    return smooth(own, other, low, high)


def solution(mesh):
    rows, cols, planes = mesh.devices.shape
    split = jax.sharding.Mesh(mesh.devices.reshape(2, rows // 2, cols, planes), ("yh", "zc", "col", "gz"))
    return jax.shard_map(
        shards,
        mesh=split,
        in_specs=(P(None, None, "gz", ("yh", "zc", "col"), None),),
        out_specs=P("gz", "col", ("yh", "zc")),
        check_vma=False,
    )
```

profile of v0, /device:TPU:0, one launch (start us, length us, event | category | flops | bytes accessed | tf_op | source)
XLA Modules:
  0.0 141.7 jit_solution(4752709466255709712)
XLA Ops:
  0.0 1.9 %copy-done = bf16[3,2,1,64,4096]{4,3,2,1,0:T(8,128)(2,1)S(1)} copy-done((bf16[3,2,1,64,4096]{4,3,2,1,0:T(8,128)(2,1)S(1)}, bf16[3,2,1,64,4096]{4,3,2,1,0:T(8,128)(2,1)}, u32[]{:S(2)}) %copy-start) | copy-done | bytes 3145752
  1.9 0.9 copy-done.3
  2.8 0.8 copy-done.7
  3.6 7.1 %lines_curl_x_curl_y.1 = (bf16[32,128,128]{2,1,0:T(8,128)(2,1)S(1)}, bf16[32,128,128]{2,1,0:T(8,128)(2,1)}) custom-call(bf16[3,2,64,4096]{3,2,1,0:T(8,128)(2,1)S(1)} %bitcast.3, bf16[3,2,64,4096]{3,2,1,0:T(8,128)(2,1)S(1)} %bitcast.4, bf16[3,2,64,4096]{3,2,1,0:T(8,128)(2,1)S(1)} %bitcast.5, bf16[512,256]{1,0:T(8,128)(2,1)S(1)} %copy-done.3, ...), custom_call_target="tpu_custom_call" | custom-call | flops 1073741824 | bytes 4194304 | tf_op jit(solution)/shard_map/lines_curl_x_curl_y/pallas_call | solution.py:177
  10.7 3.3 %collective-permute-start = (bf16[32,128,128]{2,1,0:T(8,128)(2,1)}, bf16[32,128,128]{2,1,0:T(8,128)(2,1)S(1)}, u32[]{:S(2)}, u32[]{:S(2)}) collective-permute-start(bf16[32,128,128]{2,1,0:T(8,128)(2,1)} %get-tuple-element.14), channel_id=1, source_target_pairs={{0,64},{1,65},{64,0},{65,1},{2,66},{3,67},{66,2},{67,3},{4,68},{5,... | collective-permute-start | bytes 3145736 | tf_op jit(solution)/shard_map/ppermute | solution.py:463
  14.0 4.3 %lines_curl_z.1.refs_4_ = bf16[32,128,128]{2,1,0:T(8,128)(2,1)} custom-call(bf16[3,2,64,4096]{3,2,1,0:T(8,128)(2,1)S(1)} %bitcast.6, bf16[3,2,64,4096]{3,2,1,0:T(8,128)(2,1)S(1)} %bitcast.7, bf16[512,256]{1,0:T(8,128)(2,1)S(1)} %copy-done.3, f32[2,32,128]{2,1,0:T(8,128)S(1)} %copy-done.7, bf16[32,128,128]{2,1,0:T(8,128)(2,1)S(1)} %get-tuple-element.13.refs_4_.own), custom_call_target="tpu_custom_call" | custom-call | flops 1073741824 | bytes 4194304 | tf_op jit(solution)/shard_map/lines_curl_z/pallas_call | solution.py:177
  18.3 8.3 %lines_u_v.1 = (bf16[32,128,128]{2,1,0:T(8,128)(2,1)}, bf16[32,128,128]{2,1,0:T(8,128)(2,1)}) custom-call(bf16[3,2,64,4096]{3,2,1,0:T(8,128)(2,1)} %bitcast.1, bf16[3,2,64,4096]{3,2,1,0:T(8,128)(2,1)} %bitcast.2, bf16[512,256]{1,0:T(8,128)(2,1)S(1)} %copy-done.4, f32[2,32,128]{2,1,0:T(8,128)S(1)} %copy-done.8, bf16[32,128,128]{2,1,0:T(8,128)(2,1)} %lines_curl_z.1.refs_4_), custom_call_target="tpu_custom_call" | custom-call | flops 1073741824 | bytes 4194304 | tf_op jit(solution)/shard_map/lines_u_v/pallas_call | solution.py:177
  26.6 0.7 collective-permute-start.1
  27.3 0.4 collective-permute-start.2
  27.7 8.2 %all-to-all-start.1 = ((bf16[32,128,128]{2,1,0:T(8,128)(2,1)}), bf16[32,128,128]{2,1,0:T(8,128)(2,1)S(1)}, u32[]{:S(2)}, u32[]{:S(2)}) async-start(bf16[32,128,128]{2,1,0:T(8,128)(2,1)} %lines_curl_z.1.refs_4_), calls=%async_computation.1 | async-start | bytes 2097152 | tf_op jit(solution)/shard_map/all_to_all | solution.py:471
  35.8 2.7 %collective-permute-done.came = bf16[32,128,128]{2,1,0:T(8,128)(2,1)S(1)} collective-permute-done((bf16[32,128,128]{2,1,0:T(8,128)(2,1)}, bf16[32,128,128]{2,1,0:T(8,128)(2,1)S(1)}, u32[]{:S(2)}, u32[]{:S(2)}) %collective-permute-start) | collective-permute-done | bytes 1048608 | tf_op jit(solution)/shard_map/ppermute | solution.py:463
  38.5 21.9 %collective-permute-done.1.near = bf16[32,128,128]{2,1,0:T(8,128)(2,1)} collective-permute-done((bf16[32,128,128]{2,1,0:T(8,128)(2,1)}, bf16[32,128,128]{2,1,0:T(8,128)(2,1)}, u32[]{:S(2)}, u32[]{:S(2)}) %collective-permute-start.1) | collective-permute-done | bytes 1048608 | tf_op jit(solution)/shard_map/ppermute | solution.py:463
  60.4 0.0 collective-permute-done.2.across
  60.4 4.0 %meet.1 = bf16[32,256,128]{2,1,0:T(8,128)(2,1)} custom-call(bf16[32,128,128]{2,1,0:T(8,128)(2,1)S(1)} %get-tuple-element.13.refs_4_.own, bf16[32,128,128]{2,1,0:T(8,128)(2,1)S(1)} %collective-permute-done.came, bf16[32,128,128]{2,1,0:T(8,128)(2,1)} %collective-permute-done.1.near, bf16[32,128,128]{2,1,0:T(8,128)(2,1)} %collective-permute-done.2.across), custom_call_target="tpu_custom_call" | custom-call | flops 1048576 | bytes 4194304 | tf_op jit(solution)/shard_map/meet/pallas_call | solution.py:205
  64.4 0.0 all-to-all-done.1.own
  64.4 8.3 %all-to-all-start = ((bf16[32,256,128]{2,1,0:T(8,128)(2,1)}), bf16[32,256,128]{2,1,0:T(8,128)(2,1)S(1)}, u32[]{:S(2)}, u32[]{:S(2)}) async-start(bf16[32,256,128]{2,1,0:T(8,128)(2,1)} %meet.1), calls=%async_computation | async-start | bytes 4194304 | tf_op jit(solution)/shard_map/all_to_all | solution.py:471
  72.8 3.1 %collective-permute-start.3 = (bf16[32,64,128]{2,1,0:T(8,128)(2,1)S(1)}, bf16[32,64,128]{2,1,0:T(8,128)(2,1)S(1)}, u32[]{:S(2)}, u32[]{:S(2)}) collective-permute-start(bf16[32,64,128]{2,1,0:T(8,128)(2,1)S(1)} %slice.4), channel_id=1, source_target_pairs={{0,64},{1,65},{64,0},{65,1},{2,66},{3,67},{66,2},{67,3},{4,68},{5,... | collective-permute-start | bytes 1572872 | tf_op jit(solution)/shard_map/ppermute | solution.py:463
  75.8 12.8 %collective-permute-done.3.came = bf16[32,64,128]{2,1,0:T(8,128)(2,1)S(1)} collective-permute-done((bf16[32,64,128]{2,1,0:T(8,128)(2,1)S(1)}, bf16[32,64,128]{2,1,0:T(8,128)(2,1)S(1)}, u32[]{:S(2)}, u32[]{:S(2)}) %collective-permute-start.3) | collective-permute-done | bytes 524320 | tf_op jit(solution)/shard_map/ppermute | solution.py:463
  88.6 1.6 %y_first.1.before = f32[128,2048]{1,0:T(8,128)S(1)} custom-call(bf16[32,128,128]{2,1,0:T(8,128)(2,1)S(1)} %all-to-all-done.1.own, bf16[32,64,128]{2,1,0:T(8,128)(2,1)S(1)} %collective-permute-done.3.came, bf16[256,256]{1,0:T(8,128)(2,1)S(1)} %copy-done.5, f32[2,64,128]{2,1,0:T(8,128)S(1)} %copy-done.6), custom_call_target="tpu_custom_call" | custom-call | flops 268435456 | bytes 4194304 | tf_op jit(solution)/shard_map/y_first/pallas_call | solution.py:289
  90.2 0.0 copy-start.1
  90.2 1.0 copy-done.1
  91.2 9.0 %all-to-all-done.source = bf16[32,256,128]{2,1,0:T(8,128)(2,1)S(1)} async-done(((bf16[32,256,128]{2,1,0:T(8,128)(2,1)}), bf16[32,256,128]{2,1,0:T(8,128)(2,1)S(1)}, u32[]{:S(2)}, u32[]{:S(2)}) %all-to-all-start) | async-done | bytes 2097184 | tf_op jit(solution)/shard_map/all_to_all | solution.py:471
  100.2 1.2 copy-done.2
  101.4 1.6 %y_next.1.before = f32[128,2048]{1,0:T(8,128)S(1)} custom-call(bf16[32,256,128]{2,1,0:T(8,128)(2,1)S(1)} %all-to-all-done.source, f32[128,2048]{1,0:T(8,128)S(1)} %copy-done.2, bf16[256,256]{1,0:T(8,128)(2,1)S(1)} %copy-done.5, f32[2,64,128]{2,1,0:T(8,128)S(1)} %copy-done.6), custom_call_target="tpu_custom_call" | custom-call | flops 268435456 | bytes 4194304 | tf_op jit(solution)/shard_map/y_next/pallas_call | solution.py:289
  103.0 1.7 %y_last.1 = bf16[8,32,2304]{2,1,0:T(8,128)(2,1)S(1)} custom-call(bf16[32,256,128]{2,1,0:T(8,128)(2,1)S(1)} %all-to-all-done.source, f32[128,2048]{1,0:T(8,128)S(1)} %y_next.1.before, bf16[256,256]{1,0:T(8,128)(2,1)S(1)} %copy-done.5, f32[2,64,128]{2,1,0:T(8,128)S(1)} %copy-done.6), custom_call_target="tpu_custom_call" | custom-call | flops 268435456 | bytes 4194304 | tf_op jit(solution)/shard_map/y_last/pallas_call | solution.py:289
  104.7 21.6 %all_to_all.15.field = bf16[8,32,2304]{2,1,0:T(8,128)(2,1)S(1)} all-to-all(bf16[8,32,2304]{2,1,0:T(8,128)(2,1)S(1)} %y_last.1), channel_id=1, replica_groups=mesh['yh'=2,'zc'=8,'col'=4,'gz'=2] {'gz','col'}, dimensions={0} | all-to-all | bytes 2359296 | tf_op jit(solution)/shard_map/all_to_all | solution.py:471
  126.4 0.1 edges.1
  126.5 0.1 collective-permute-start.4
  126.6 5.3 %collective-permute-start.5 = (bf16[2,16,640]{2,1,0:T(8,128)(2,1)S(1)}, bf16[2,16,640]{2,1,0:T(8,128)(2,1)S(1)}, u32[]{:S(2)}, u32[]{:S(2)}) collective-permute-start(bf16[2,16,640]{2,1,0:T(8,128)(2,1)S(1)} %get-tuple-element.20), channel_id=1, source_target_pairs={{0,120},{8,0},{16,8},{24,16},{32,24},{40,32},{48,40},{56,48},{64,5... | collective-permute-start | bytes 122888 | tf_op jit(solution)/shard_map/ppermute | solution.py:454
  132.0 2.0 %regroup.1 = (f32[72,16,256]{2,1,0:T(8,128)S(1)}, f32[72,16,256]{2,1,0:T(8,128)S(1)}) custom-call(bf16[8,32,2304]{2,1,0:T(8,128)(2,1)S(1)} %all_to_all.15.field), custom_call_target="tpu_custom_call" | custom-call | flops 16777216 | bytes 8388608 | tf_op jit(solution)/shard_map/regroup/pallas_call | solution.py:344
  133.9 0.0 collective-permute-done.5.high
  133.9 7.7 %smooth.1 = f32[1,1024,256]{2,1,0:T(8,128)} custom-call(f32[72,16,256]{2,1,0:T(8,128)S(1)} %get-tuple-element.17.own, f32[72,16,256]{2,1,0:T(8,128)S(1)} %get-tuple-element.18.other, bf16[2,16,640]{2,1,0:T(8,128)(2,1)S(1)} %collective-permute-done.4.low, bf16[2,16,640]{2,1,0:T(8,128)(2,1)S(1)} %collective-permute-done.5.high), custom_call_target="tpu_custom_call" | custom-call | tf_op jit(solution)/shard_map/smooth/pallas_call | solution.py:438
  (14 shorter events, 0.1 us)
Async XLA Ops:
  0.0 1.9 %copy-start = (bf16[3,2,1,64,4096]{4,3,2,1,0:T(8,128)(2,1)S(1)}, bf16[3,2,1,64,4096]{4,3,2,1,0:T(8,128)(2,1)}, u32[]{:S(2)}) copy-start(bf16[3,2,1,64,4096]{4,3,2,1,0:T(8,128)(2,1)} %param.5) | copy-start | bytes 9437188
  1.9 0.9 copy-start.3
  2.8 0.8 copy-start.7
  10.7 27.8 %collective-permute-start = (bf16[32,128,128]{2,1,0:T(8,128)(2,1)}, bf16[32,128,128]{2,1,0:T(8,128)(2,1)S(1)}, u32[]{:S(2)}, u32[]{:S(2)}) collective-permute-start(bf16[32,128,128]{2,1,0:T(8,128)(2,1)} %get-tuple-element.14), channel_id=1, source_target_pairs={{0,64},{1,65},{64,0},{65,1},{2,66},{3,67},{66,2},{67,3},{4,68},{5,... | collective-permute-start | bytes 3145736 | tf_op jit(solution)/shard_map/ppermute | solution.py:463
  14.0 4.3 %copy-start.4 = (bf16[512,256]{1,0:T(8,128)(2,1)S(1)}, bf16[512,256]{1,0:T(8,128)(2,1)}, u32[]{:S(2)}) copy-start(bf16[512,256]{1,0:T(8,128)(2,1)} %constant.8.clone.refs_3_.refs_2_) | copy-start | bytes 786436
  14.0 4.3 %copy-start.8 = (f32[2,32,128]{2,1,0:T(8,128)S(1)}, f32[2,32,128]{2,1,0:T(8,128)}, u32[]{:S(2)}) copy-start(f32[2,32,128]{2,1,0:T(8,128)} %constant.9.clone.refs_4_.refs_3_) | copy-start | bytes 98308
  26.6 33.8 %collective-permute-start.1 = (bf16[32,128,128]{2,1,0:T(8,128)(2,1)}, bf16[32,128,128]{2,1,0:T(8,128)(2,1)}, u32[]{:S(2)}, u32[]{:S(2)}) collective-permute-start(bf16[32,128,128]{2,1,0:T(8,128)(2,1)} %get-tuple-element.15), channel_id=1, source_target_pairs={{0,1},{1,0},{64,65},{65,64},{2,3},{3,2},{66,67},{67,66},{4,5},{5,4... | collective-permute-start | bytes 3145736 | tf_op jit(solution)/shard_map/ppermute | solution.py:463
  27.3 33.1 %collective-permute-start.2 = (bf16[32,128,128]{2,1,0:T(8,128)(2,1)}, bf16[32,128,128]{2,1,0:T(8,128)(2,1)}, u32[]{:S(2)}, u32[]{:S(2)}) collective-permute-start(bf16[32,128,128]{2,1,0:T(8,128)(2,1)} %get-tuple-element.16), channel_id=1, source_target_pairs={{0,65},{1,64},{64,1},{65,0},{2,67},{3,66},{66,3},{67,2},{4,69},{5,... | collective-permute-start | bytes 3145736 | tf_op jit(solution)/shard_map/ppermute | solution.py:463
  27.7 36.7 %all-to-all-start.1 = ((bf16[32,128,128]{2,1,0:T(8,128)(2,1)}), bf16[32,128,128]{2,1,0:T(8,128)(2,1)S(1)}, u32[]{:S(2)}, u32[]{:S(2)}) async-start(bf16[32,128,128]{2,1,0:T(8,128)(2,1)} %lines_curl_z.1.refs_4_), calls=%async_computation.1 | async-start | bytes 2097152 | tf_op jit(solution)/shard_map/all_to_all | solution.py:471
  64.4 24.2 %copy-start.5 = (bf16[256,256]{1,0:T(8,128)(2,1)S(1)}, bf16[256,256]{1,0:T(8,128)(2,1)}, u32[]{:S(2)}) copy-start(bf16[256,256]{1,0:T(8,128)(2,1)} %constant.10.clone.matrix) | copy-start | bytes 393220
  64.4 24.2 %copy-start.6 = (f32[2,64,128]{2,1,0:T(8,128)S(1)}, f32[2,64,128]{2,1,0:T(8,128)}, u32[]{:S(2)}) copy-start(f32[2,64,128]{2,1,0:T(8,128)} %constant.11.clone.twist) | copy-start | bytes 196612
  64.4 35.8 %all-to-all-start = ((bf16[32,256,128]{2,1,0:T(8,128)(2,1)}), bf16[32,256,128]{2,1,0:T(8,128)(2,1)S(1)}, u32[]{:S(2)}, u32[]{:S(2)}) async-start(bf16[32,256,128]{2,1,0:T(8,128)(2,1)} %meet.1), calls=%async_computation | async-start | bytes 4194304 | tf_op jit(solution)/shard_map/all_to_all | solution.py:471
  72.8 15.9 %collective-permute-start.3 = (bf16[32,64,128]{2,1,0:T(8,128)(2,1)S(1)}, bf16[32,64,128]{2,1,0:T(8,128)(2,1)S(1)}, u32[]{:S(2)}, u32[]{:S(2)}) collective-permute-start(bf16[32,64,128]{2,1,0:T(8,128)(2,1)S(1)} %slice.4), channel_id=1, source_target_pairs={{0,64},{1,65},{64,0},{65,1},{2,66},{3,67},{66,2},{67,3},{4,68},{5,... | collective-permute-start | bytes 1572872 | tf_op jit(solution)/shard_map/ppermute | solution.py:463
  90.2 1.0 copy-start.1
  100.2 1.2 copy-start.2
  126.5 7.4 %collective-permute-start.4 = (bf16[2,16,640]{2,1,0:T(8,128)(2,1)S(1)}, bf16[2,16,640]{2,1,0:T(8,128)(2,1)S(1)}, u32[]{:S(2)}, u32[]{:S(2)}) collective-permute-start(bf16[2,16,640]{2,1,0:T(8,128)(2,1)S(1)} %get-tuple-element.19), channel_id=1, source_target_pairs={{0,8},{8,16},{16,24},{24,32},{32,40},{40,48},{48,56},{56,64},{64,7... | collective-permute-start | bytes 122888 | tf_op jit(solution)/shard_map/ppermute | solution.py:454
  126.6 7.3 %collective-permute-start.5 = (bf16[2,16,640]{2,1,0:T(8,128)(2,1)S(1)}, bf16[2,16,640]{2,1,0:T(8,128)(2,1)S(1)}, u32[]{:S(2)}, u32[]{:S(2)}) collective-permute-start(bf16[2,16,640]{2,1,0:T(8,128)(2,1)S(1)} %get-tuple-element.20), channel_id=1, source_target_pairs={{0,120},{8,0},{16,8},{24,16},{32,24},{40,32},{48,40},{56,48},{64,5... | collective-permute-start | bytes 122888 | tf_op jit(solution)/shard_map/ppermute | solution.py:454
where the time goes:
time: 144 us; the launch traced here: 142 us
  waiting for transfers between devices  46.3 us (32%)
  Pallas kernels  38.5 us (27%)
  starting transfers between devices  29.3 us (20%)
  blocking collectives  21.6 us (15%)
  local copies, waits for them, and re-layouts  5.84 us (4%)
    ppermute x4, waiting for transfers between devices, between_y(): return lax.ppermute(value, ('yh', 'gz'), pairs)  37.4 us
    all_to_all x1, blocking collectives, exchanged(): return lax.all_to_all(array, axes, split_axis=0, concat_axis=0, tiled=True)  21.6 us
    pallas_call x3, Pallas kernels, x_transform(): pl.pallas_call(lambda *refs: x_kernel(fields, rows_local, *refs), grid=(r...  19.7 us
    all_to_all x2, starting transfers between devices, exchanged(): return lax.all_to_all(array, axes, split_axis=0, concat_axis=0, tiled=True)  16.5 us
    all_to_all x2, waiting for transfers between devices, exchanged(): return lax.all_to_all(array, axes, split_axis=0, concat_axis=0, tiled=True)  8.97 us
    pallas_call x1, Pallas kernels, smooth(): pl.pallas_call(smooth_kernel, out_shape=jax.ShapeDtypeStruct((1, 1024, 25...  7.71 us
    ppermute x4, starting transfers between devices, between_y(): return lax.ppermute(value, ('yh', 'gz'), pairs)  7.4 us
    unnamed x18, local copies, waits for them, and re-layouts  5.8 us
  transfers between devices with their start and end apart: 8, of which 4 were waited for; matrix products, arithmetic and copies ran while one was open for 0% of the time, Pallas kernels for 14%

commit v1 on v0

--- a/solution.py
+++ b/solution.py
@@ -10,40 +10,41 @@
 
 GRID = 4096
 RELAX = 0.15
-VMEM_LIMIT = 48 * 1024 * 1024
+VMEM_LIMIT = 28 * 1024 * 1024
+PAD = 72
 NT = (((1,), (1,)), ((), ()))
+
+
+def cos_sin(rows, columns, period):
+    turn = rows[:, None] * columns[None, :] % period
+    angle = turn.astype(jnp.float32) * (2.0 * math.pi / period)
+    return jnp.cos(angle), jnp.sin(angle)
 
 
 def split_bf16(table):
     high = table.astype(jnp.bfloat16)
-    low = (table - high.astype(np.float64)).astype(jnp.bfloat16)
-    return np.concatenate([high, low], axis=0)
+    low = (table - high.astype(jnp.float32)).astype(jnp.bfloat16)
+    return jnp.concatenate([high, low], axis=0)
 
 
 def tables():
-    k = np.arange(128)
+    k, j, b = jnp.arange(128), jnp.arange(64), jnp.arange(64)
     blocks = []
     for s in range(2):
-        angle = 2 * np.pi * ((np.arange(64)[:, None] * 2 + s) * k[None, :] % 128) / 128
-        c, d = np.cos(angle), np.sin(angle)
-        blocks.append(np.concatenate([c, -d], axis=1))
-        blocks.append(np.concatenate([d, c], axis=1))
-    x_matrix = split_bf16(np.concatenate(blocks, axis=0))
-    angle = 2 * np.pi * (np.arange(32)[:, None] * k[None, :]) / 4096
-    x_twist = np.stack([np.cos(angle), np.sin(angle)]).astype(np.float32) / 64
-    j = np.arange(64)
-    angle = 2 * np.pi * (j[:, None] * j[None, :] % 64) / 64
-    zero = np.zeros((64, 64))
-    c, d = np.cos(angle), -np.sin(angle)
+        c, d = cos_sin(b * 2 + s, k, 128)
+        blocks.append(jnp.concatenate([c, -d], axis=1))
+        blocks.append(jnp.concatenate([d, c], axis=1))
+    x_matrix = split_bf16(jnp.concatenate(blocks, axis=0))
+    x_twist = jnp.stack(cos_sin(jnp.arange(32), k, 4096)) / 64
+    zero = jnp.zeros((64, 64), jnp.float32)
+    c, d = cos_sin(j, j, 64)
     y_matrix = split_bf16(
-        np.concatenate(
-            [np.concatenate([c, zero, d, zero], axis=1), np.concatenate([zero, c, zero, d], axis=1)], axis=0
+        jnp.concatenate(
+            [jnp.concatenate([c, zero, -d, zero], axis=1), jnp.concatenate([zero, c, zero, -d], axis=1)], axis=0
         )
     )
-    angle = 2 * np.pi * (j[:, None] * j[None, :]) / 4096
-    y_twist = np.stack([np.cos(angle), np.sin(angle)]).astype(np.float32) / 64
-    y_twist = np.concatenate([y_twist, y_twist], axis=2)
-    return x_matrix, x_twist, y_matrix, y_twist
+    y_twist = jnp.stack(cos_sin(j, j, 4096)) / 64
+    return x_matrix, x_twist, y_matrix, jnp.concatenate([y_twist, y_twist], axis=2)
 
 
 def turned(value, num, den):
@@ -152,13 +153,13 @@
                     for s in range(2):
                         for c in range(2):
                             at = (s * 2 + c) * 64
-                            spread[pl.ds(c * 32 + s * 16 + n16, 64, stride=64), :] = got[
+                            spread[pl.ds(c * 32 + s * 16 + n16, 64, stride=PAD), :] = got[
                                 at : at + 64, half * 128 : half * 128 + 128
                             ]
             for half in range(2):
-                first = (lax.axis_index("yh") + half) % 2 * 2048
+                first = (lax.axis_index("yh") + half) % 2 * (32 * PAD)
                 for b in range(32):
-                    at = pl.ds(pl.multiple_of(first + b * 64, 64), 64)
+                    at = pl.ds(pl.multiple_of(first + b * PAD, 8), 64)
                     block = spread[at, :].astype(jnp.bfloat16)
                     if n_out == 1:
                         outs[0][b, half * 64 : half * 64 + 64, :] = block
@@ -183,7 +184,7 @@
         scratch_shapes=[
             pltpu.VMEM((2, 32, 16, 128), jnp.float32),
             pltpu.VMEM((len(fields), 2048, 256), jnp.bfloat16),
-            pltpu.VMEM((4096, 128), jnp.float32),
+            pltpu.VMEM((64 * PAD, 128), jnp.float32),
         ],
         compiler_params=pltpu.CompilerParams(vmem_limit_bytes=VMEM_LIMIT),
         cost_estimate=pl.CostEstimate(flops=2**30, bytes_accessed=2**22, transcendentals=0),
@@ -204,9 +205,9 @@
 def meet(own, came, near, across):
     return pl.pallas_call(
         meet_kernel,
-        grid=(4,),
-        in_specs=[pl.BlockSpec((8, 128, 128), lambda i: (i, 0, 0))] * 4,
-        out_specs=pl.BlockSpec((8, 256, 128), lambda i: (i, 0, 0)),
+        grid=(2,),
+        in_specs=[pl.BlockSpec((16, 128, 128), lambda i: (i, 0, 0))] * 4,
+        out_specs=pl.BlockSpec((16, 256, 128), lambda i: (i, 0, 0)),
         out_shape=jax.ShapeDtypeStruct((32, 256, 128), jnp.bfloat16),
         compiler_params=pltpu.CompilerParams(vmem_limit_bytes=VMEM_LIMIT),
         cost_estimate=pl.CostEstimate(flops=2**20, bytes_accessed=2**22, transcendentals=0),
@@ -255,18 +256,15 @@
     y_squares(((own, 0), (came, 0)), matrix, twist, stage, lines, add)
 
 
-def y_next(source, before, matrix, twist, out, stage, lines):
-    def add(at, square):
-        out[at] = before[at] + square
-
-    y_squares(((source, 0), (source, 64)), matrix, twist, stage, lines, add)
-
-
 def y_last(source, before, matrix, twist, out, stage, lines, total):
     def add(at, square):
-        total[at] = jnp.sqrt(before[at] + square)
-
-    y_squares(((source, 128), (source, 192)), matrix, twist, stage, lines, add)
+        total[at] = before[at] + square
+
+    def finish(at, square):
+        total[at] = jnp.sqrt(total[at] + square)
+
+    y_squares(((source, 0), (source, 64)), matrix, twist, stage, lines, add)
+    y_squares(((source, 128), (source, 192)), matrix, twist, stage, lines, finish)
 
     def put(h, tile, value):
         value = value.astype(jnp.bfloat16)
@@ -425,13 +423,14 @@
         value = beside(lambda i: work[1, i], y, center)[:, 0:256]
         value = own[y] * own_c[0] + other[y] * other_c[0] + value
         for half in range(2):
-            spread[pl.ds(half * 1024 + y - 4, 16, stride=64), :] = value[:, half * 128 : half * 128 + 128]
-
-    each(2, 70, 4, first)
-    each(3, 69, 6, second)
-    each(4, 68, 4, third)
+            spread[pl.ds(half * 16 * PAD + y - 4, 16, stride=PAD), :] = value[:, half * 128 : half * 128 + 128]
+
+    each(2, 70, 34, first)
+    each(3, 69, 33, second)
+    each(4, 68, 32, third)
     for half in range(2):
-        out[0, :, half * 128 : half * 128 + 128] = spread[pl.ds(half * 1024, 1024), :]
+        for k in range(16):
+            out[0, k * 64 : k * 64 + 64, half * 128 : half * 128 + 128] = spread[pl.ds((half * 16 + k) * PAD, 64), :]
 
 
 def smooth(own, other, low, high):
@@ -442,7 +441,7 @@
             pltpu.VMEM((72, 16, 128), jnp.float32),
             pltpu.VMEM((72, 16, 128), jnp.float32),
             pltpu.VMEM((2, 72, 16, 384), jnp.float32),
-            pltpu.VMEM((2048, 128), jnp.float32),
+            pltpu.VMEM((32 * PAD, 128), jnp.float32),
         ],
         compiler_params=pltpu.CompilerParams(vmem_limit_bytes=VMEM_LIMIT),
         name="smooth",
@@ -464,7 +463,7 @@
 
 
 def shards(velocity_hat):
-    x_matrix, x_twist, y_matrix, y_twist = (jnp.asarray(t) for t in tables())
+    x_matrix, x_twist, y_matrix, y_twist = tables()
     parts = velocity_hat.reshape((3, 2) + velocity_hat.shape[3:])
 
     def exchanged(array, axes):
@@ -483,7 +482,6 @@
     came_2 = between_y(line_2[:, 64:], lambda y_hi, gz: (1 - y_hi, gz))
     both = exchanged(meet(curl_own, came, near, across), ("zc", "col"))
     squares = y_transform(y_first, (line_2, came_2), y_matrix, y_twist)
-    squares = y_transform(y_next, (both, squares), y_matrix, y_twist)
     magnitude = y_transform(y_last, (both, squares), y_matrix, y_twist)
     field = exchanged(magnitude, ("gz", "col"))
     last, first = edges(field)

time: 144 us -> 136 us (0.944)
  Pallas kernels: 38.5 us -> 28.1 us
  waiting for transfers between devices: 46.3 us -> 49.8 us
  local copies, waits for them, and re-layouts: 5.84 us -> 4.12 us
    pallas_call x3, Pallas kernels: 19.7 us -> 14 us  [x_transform(): pl.pallas_call(lambda *refs: x_kernel(fields, rows_local, *refs), grid=(r...]
    ppermute x4, waiting for transfers between devices: 37.4 us -> 41 us  [between_y(): return lax.ppermute(value, ('yh', 'gz'), pairs)]
    pallas_call x1, Pallas kernels: 7.71 us -> 4.5 us  [smooth(): pl.pallas_call(smooth_kernel, out_shape=jax.ShapeDtypeStruct((1, 1024, 25...]
    unnamed x18 -> x6, local copies, waits for them, and re-layouts: 5.8 us -> 4.07 us
    pallas_call x3 -> x2, Pallas kernels: 4.92 us -> 4.68 us  [y_transform(): pl.pallas_call(kernel, out_shape=jax.ShapeDtypeStruct((8, 32, 2304), jnp....]
  transfers between devices with their start and end apart: 8 -> 8, of which waited for: 4 -> 4; matrix products, arithmetic and copies ran while one was open for 0% -> 0% of each run, Pallas kernels for 14% -> 11%
where the time goes in v1:
time: 136 us; the launch traced here: 134 us
  waiting for transfers between devices  49.8 us (37%)
  starting transfers between devices  29 us (21%)
  Pallas kernels  28.1 us (21%)
  blocking collectives  21.6 us (16%)
  local copies, waits for them, and re-layouts  4.12 us (3%)
    ppermute x4, waiting for transfers between devices, between_y(): return lax.ppermute(value, ('yh', 'gz'), pairs)  41 us
    all_to_all x1, blocking collectives, exchanged(): return lax.all_to_all(array, axes, split_axis=0, concat_axis=0, tiled=True)  21.6 us
    all_to_all x2, starting transfers between devices, exchanged(): return lax.all_to_all(array, axes, split_axis=0, concat_axis=0, tiled=True)  16.3 us
    pallas_call x3, Pallas kernels, x_transform(): pl.pallas_call(lambda *refs: x_kernel(fields, rows_local, *refs), grid=(r...  14 us
    all_to_all x2, waiting for transfers between devices, exchanged(): return lax.all_to_all(array, axes, split_axis=0, concat_axis=0, tiled=True)  8.87 us
    ppermute x4, starting transfers between devices, between_y(): return lax.ppermute(value, ('yh', 'gz'), pairs)  7.22 us
    ppermute x2, starting transfers between devices, ring(): lax.ppermute(value, axis, [(i, (i + steps) % count) for i in range(count)])  5.42 us
    pallas_call x2, Pallas kernels, y_transform(): pl.pallas_call(kernel, out_shape=jax.ShapeDtypeStruct((8, 32, 2304), jnp....  4.68 us
  transfers between devices with their start and end apart: 8, of which 4 were waited for; matrix products, arithmetic and copies ran while one was open for 0% of the time, Pallas kernels for 11%

profile of v1, /device:TPU:0, one launch (start us, length us, event | category | flops | bytes accessed | tf_op | source)
XLA Modules:
  0.0 134.0 jit_solution(14998753084965269700)
XLA Ops:
  0.0 0.3 fusion.39
  0.4 0.1 fusion.41
  0.5 1.9 %copy-done = bf16[3,2,1,64,4096]{4,3,2,1,0:T(8,128)(2,1)S(1)} copy-done((bf16[3,2,1,64,4096]{4,3,2,1,0:T(8,128)(2,1)S(1)}, bf16[3,2,1,64,4096]{4,3,2,1,0:T(8,128)(2,1)}, u32[]{:S(2)}) %copy-start) | copy-done | bytes 3145752
  2.4 5.4 %lines_curl_x_curl_y.1 = (bf16[32,128,128]{2,1,0:T(8,128)(2,1)S(1)}, bf16[32,128,128]{2,1,0:T(8,128)(2,1)}) custom-call(bf16[3,2,64,4096]{3,2,1,0:T(8,128)(2,1)S(1)} %bitcast.1, bf16[3,2,64,4096]{3,2,1,0:T(8,128)(2,1)S(1)} %bitcast.2, bf16[3,2,64,4096]{3,2,1,0:T(8,128)(2,1)S(1)} %bitcast.3, bf16[512,256]{1,0:T(8,128)(2,1)S(1)} %pad_maximum_fusion.refs_3_.refs_2_, ...), custom_call_target="tpu_custom_call" | custom-call | flops 1073741824 | bytes 4194304 | tf_op jit(solution)/shard_map/lines_curl_x_curl_y/pallas_call | solution.py:178
  7.8 3.3 %collective-permute-start = (bf16[32,128,128]{2,1,0:T(8,128)(2,1)}, bf16[32,128,128]{2,1,0:T(8,128)(2,1)S(1)}, u32[]{:S(2)}, u32[]{:S(2)}) collective-permute-start(bf16[32,128,128]{2,1,0:T(8,128)(2,1)} %get-tuple-element.14), channel_id=1, source_target_pairs={{0,64},{1,65},{64,0},{65,1},{2,66},{3,67},{66,2},{67,3},{4,68},{5,... | collective-permute-start | bytes 3145736 | tf_op jit(solution)/shard_map/ppermute | solution.py:462
  11.1 3.5 %lines_curl_z.1.refs_4_ = bf16[32,128,128]{2,1,0:T(8,128)(2,1)} custom-call(bf16[3,2,64,4096]{3,2,1,0:T(8,128)(2,1)S(1)} %bitcast.4, bf16[3,2,64,4096]{3,2,1,0:T(8,128)(2,1)S(1)} %bitcast.5, bf16[512,256]{1,0:T(8,128)(2,1)S(1)} %pad_maximum_fusion.refs_3_.refs_2_, f32[2,32,128]{2,1,0:T(8,128)S(1)} %maximum_multiply_fusion.1.refs_4_.refs_3_, ...), custom_call_target="tpu_custom_call" | custom-call | flops 1073741824 | bytes 4194304 | tf_op jit(solution)/shard_map/lines_curl_z/pallas_call | solution.py:178
  14.6 5.1 %lines_u_v.1 = (bf16[32,128,128]{2,1,0:T(8,128)(2,1)}, bf16[32,128,128]{2,1,0:T(8,128)(2,1)}) custom-call(bf16[3,2,64,4096]{3,2,1,0:T(8,128)(2,1)S(1)} %bitcast.6, bf16[3,2,64,4096]{3,2,1,0:T(8,128)(2,1)S(1)} %bitcast.7, bf16[512,256]{1,0:T(8,128)(2,1)S(1)} %pad_maximum_fusion.refs_3_.refs_2_, f32[2,32,128]{2,1,0:T(8,128)S(1)} %maximum_multiply_fusion.1.refs_4_.refs_3_, ...), custom_call_target="tpu_custom_call" | custom-call | flops 1073741824 | bytes 4194304 | tf_op jit(solution)/shard_map/lines_u_v/pallas_call | solution.py:178
  19.7 0.7 collective-permute-start.1
  20.4 0.4 collective-permute-start.2
  20.8 8.2 %all-to-all-start.1 = ((bf16[32,128,128]{2,1,0:T(8,128)(2,1)}), bf16[32,128,128]{2,1,0:T(8,128)(2,1)S(1)}, u32[]{:S(2)}, u32[]{:S(2)}) async-start(bf16[32,128,128]{2,1,0:T(8,128)(2,1)} %lines_curl_z.1.refs_4_), calls=%async_computation.1 | async-start | bytes 2097152 | tf_op jit(solution)/shard_map/all_to_all | solution.py:470
  29.0 6.7 %collective-permute-done.came = bf16[32,128,128]{2,1,0:T(8,128)(2,1)S(1)} collective-permute-done((bf16[32,128,128]{2,1,0:T(8,128)(2,1)}, bf16[32,128,128]{2,1,0:T(8,128)(2,1)S(1)}, u32[]{:S(2)}, u32[]{:S(2)}) %collective-permute-start) | collective-permute-done | bytes 1048608 | tf_op jit(solution)/shard_map/ppermute | solution.py:462
  35.6 21.9 %collective-permute-done.1.near = bf16[32,128,128]{2,1,0:T(8,128)(2,1)} collective-permute-done((bf16[32,128,128]{2,1,0:T(8,128)(2,1)}, bf16[32,128,128]{2,1,0:T(8,128)(2,1)}, u32[]{:S(2)}, u32[]{:S(2)}) %collective-permute-start.1) | collective-permute-done | bytes 1048608 | tf_op jit(solution)/shard_map/ppermute | solution.py:462
  57.5 2.8 %meet.1 = bf16[32,256,128]{2,1,0:T(8,128)(2,1)} custom-call(bf16[32,128,128]{2,1,0:T(8,128)(2,1)S(1)} %get-tuple-element.13.refs_4_.own, bf16[32,128,128]{2,1,0:T(8,128)(2,1)S(1)} %collective-permute-done.came, bf16[32,128,128]{2,1,0:T(8,128)(2,1)} %collective-permute-done.1.near, bf16[32,128,128]{2,1,0:T(8,128)(2,1)} %collective-permute-done.2.across), custom_call_target="tpu_custom_call" | custom-call | flops 1048576 | bytes 4194304 | tf_op jit(solution)/shard_map/meet/pallas_call | solution.py:206
  60.3 8.2 %all-to-all-start = ((bf16[32,256,128]{2,1,0:T(8,128)(2,1)}), bf16[32,256,128]{2,1,0:T(8,128)(2,1)S(1)}, u32[]{:S(2)}, u32[]{:S(2)}) async-start(bf16[32,256,128]{2,1,0:T(8,128)(2,1)} %meet.1), calls=%async_computation | async-start | bytes 4194304 | tf_op jit(solution)/shard_map/all_to_all | solution.py:470
  68.5 0.1 sine_negate_fusion
  68.7 0.1 subtract_convert_fusion.1
  68.8 2.9 %collective-permute-start.3 = (bf16[32,64,128]{2,1,0:T(8,128)(2,1)S(1)}, bf16[32,64,128]{2,1,0:T(8,128)(2,1)S(1)}, u32[]{:S(2)}, u32[]{:S(2)}) collective-permute-start(bf16[32,64,128]{2,1,0:T(8,128)(2,1)S(1)} %slice.4), channel_id=1, source_target_pairs={{0,64},{1,65},{64,0},{65,1},{2,66},{3,67},{66,2},{67,3},{4,68},{5,... | collective-permute-start | bytes 1572872 | tf_op jit(solution)/shard_map/ppermute | solution.py:462
  71.7 0.1 fusion.1
  71.8 0.1 fusion.29
  72.0 0.1 pad_maximum_fusion.2.twist
  72.1 12.4 %collective-permute-done.3.came = bf16[32,64,128]{2,1,0:T(8,128)(2,1)S(1)} collective-permute-done((bf16[32,64,128]{2,1,0:T(8,128)(2,1)S(1)}, bf16[32,64,128]{2,1,0:T(8,128)(2,1)S(1)}, u32[]{:S(2)}, u32[]{:S(2)}) %collective-permute-start.3) | collective-permute-done | bytes 524320 | tf_op jit(solution)/shard_map/ppermute | solution.py:462
  84.5 1.6 %y_first.1.before = f32[128,2048]{1,0:T(8,128)S(1)} custom-call(bf16[32,128,128]{2,1,0:T(8,128)(2,1)S(1)} %all-to-all-done.1.own, bf16[32,64,128]{2,1,0:T(8,128)(2,1)S(1)} %collective-permute-done.3.came, bf16[256,256]{1,0:T(8,128)(2,1)S(1)} %pad_maximum_fusion.1.matrix, f32[2,64,128]{2,1,0:T(8,128)S(1)} %pad_maximum_fusion.2.twist), custom_call_target="tpu_custom_call" | custom-call | flops 268435456 | bytes 4194304 | tf_op jit(solution)/shard_map/y_first/pallas_call | solution.py:287
  86.1 1.0 copy-done.1
  87.1 8.9 %all-to-all-done.source = bf16[32,256,128]{2,1,0:T(8,128)(2,1)S(1)} async-done(((bf16[32,256,128]{2,1,0:T(8,128)(2,1)}), bf16[32,256,128]{2,1,0:T(8,128)(2,1)S(1)}, u32[]{:S(2)}, u32[]{:S(2)}) %all-to-all-start) | async-done | bytes 2097184 | tf_op jit(solution)/shard_map/all_to_all | solution.py:470
  96.0 1.2 copy-done.2
  97.2 3.1 %y_last.1 = bf16[8,32,2304]{2,1,0:T(8,128)(2,1)S(1)} custom-call(bf16[32,256,128]{2,1,0:T(8,128)(2,1)S(1)} %all-to-all-done.source, f32[128,2048]{1,0:T(8,128)S(1)} %copy-done.2, bf16[256,256]{1,0:T(8,128)(2,1)S(1)} %pad_maximum_fusion.1.matrix, f32[2,64,128]{2,1,0:T(8,128)S(1)} %pad_maximum_fusion.2.twist), custom_call_target="tpu_custom_call" | custom-call | flops 268435456 | bytes 4194304 | tf_op jit(solution)/shard_map/y_last/pallas_call | solution.py:287
  100.3 21.6 %all_to_all.15.field = bf16[8,32,2304]{2,1,0:T(8,128)(2,1)S(1)} all-to-all(bf16[8,32,2304]{2,1,0:T(8,128)(2,1)S(1)} %y_last.1), channel_id=1, replica_groups=mesh['yh'=2,'zc'=8,'col'=4,'gz'=2] {'gz','col'}, dimensions={0} | all-to-all | bytes 2359296 | tf_op jit(solution)/shard_map/all_to_all | solution.py:470
  121.9 0.1 edges.1
  122.1 0.1 collective-permute-start.4
  122.1 5.3 %collective-permute-start.5 = (bf16[2,16,640]{2,1,0:T(8,128)(2,1)S(1)}, bf16[2,16,640]{2,1,0:T(8,128)(2,1)S(1)}, u32[]{:S(2)}, u32[]{:S(2)}) collective-permute-start(bf16[2,16,640]{2,1,0:T(8,128)(2,1)S(1)} %get-tuple-element.20), channel_id=1, source_target_pairs={{0,120},{8,0},{16,8},{24,16},{32,24},{40,32},{48,40},{56,48},{64,5... | collective-permute-start | bytes 122888 | tf_op jit(solution)/shard_map/ppermute | solution.py:453
  127.5 2.0 %regroup.1 = (f32[72,16,256]{2,1,0:T(8,128)S(1)}, f32[72,16,256]{2,1,0:T(8,128)S(1)}) custom-call(bf16[8,32,2304]{2,1,0:T(8,128)(2,1)S(1)} %all_to_all.15.field), custom_call_target="tpu_custom_call" | custom-call | flops 16777216 | bytes 8388608 | tf_op jit(solution)/shard_map/regroup/pallas_call | solution.py:342
  129.5 4.5 %smooth.1 = f32[1,1024,256]{2,1,0:T(8,128)} custom-call(f32[72,16,256]{2,1,0:T(8,128)S(1)} %get-tuple-element.17.own, f32[72,16,256]{2,1,0:T(8,128)S(1)} %get-tuple-element.18.other, bf16[2,16,640]{2,1,0:T(8,128)(2,1)S(1)} %collective-permute-done.4.low, bf16[2,16,640]{2,1,0:T(8,128)(2,1)S(1)} %collective-permute-done.5.high), custom_call_target="tpu_custom_call" | custom-call | tf_op jit(solution)/shard_map/smooth/pallas_call | solution.py:437
  (17 shorter events, 0.2 us)
Async XLA Ops:
  0.5 1.9 %copy-start = (bf16[3,2,1,64,4096]{4,3,2,1,0:T(8,128)(2,1)S(1)}, bf16[3,2,1,64,4096]{4,3,2,1,0:T(8,128)(2,1)}, u32[]{:S(2)}) copy-start(bf16[3,2,1,64,4096]{4,3,2,1,0:T(8,128)(2,1)} %param.1) | copy-start | bytes 9437188
  7.8 27.8 %collective-permute-start = (bf16[32,128,128]{2,1,0:T(8,128)(2,1)}, bf16[32,128,128]{2,1,0:T(8,128)(2,1)S(1)}, u32[]{:S(2)}, u32[]{:S(2)}) collective-permute-start(bf16[32,128,128]{2,1,0:T(8,128)(2,1)} %get-tuple-element.14), channel_id=1, source_target_pairs={{0,64},{1,65},{64,0},{65,1},{2,66},{3,67},{66,2},{67,3},{4,68},{5,... | collective-permute-start | bytes 3145736 | tf_op jit(solution)/shard_map/ppermute | solution.py:462
  19.7 37.8 %collective-permute-start.1 = (bf16[32,128,128]{2,1,0:T(8,128)(2,1)}, bf16[32,128,128]{2,1,0:T(8,128)(2,1)}, u32[]{:S(2)}, u32[]{:S(2)}) collective-permute-start(bf16[32,128,128]{2,1,0:T(8,128)(2,1)} %get-tuple-element.15), channel_id=1, source_target_pairs={{0,1},{1,0},{64,65},{65,64},{2,3},{3,2},{66,67},{67,66},{4,5},{5,4... | collective-permute-start | bytes 3145736 | tf_op jit(solution)/shard_map/ppermute | solution.py:462
  20.4 37.1 %collective-permute-start.2 = (bf16[32,128,128]{2,1,0:T(8,128)(2,1)}, bf16[32,128,128]{2,1,0:T(8,128)(2,1)}, u32[]{:S(2)}, u32[]{:S(2)}) collective-permute-start(bf16[32,128,128]{2,1,0:T(8,128)(2,1)} %get-tuple-element.16), channel_id=1, source_target_pairs={{0,65},{1,64},{64,1},{65,0},{2,67},{3,66},{66,3},{67,2},{4,69},{5,... | collective-permute-start | bytes 3145736 | tf_op jit(solution)/shard_map/ppermute | solution.py:462
  20.8 39.5 %all-to-all-start.1 = ((bf16[32,128,128]{2,1,0:T(8,128)(2,1)}), bf16[32,128,128]{2,1,0:T(8,128)(2,1)S(1)}, u32[]{:S(2)}, u32[]{:S(2)}) async-start(bf16[32,128,128]{2,1,0:T(8,128)(2,1)} %lines_curl_z.1.refs_4_), calls=%async_computation.1 | async-start | bytes 2097152 | tf_op jit(solution)/shard_map/all_to_all | solution.py:470
  60.3 35.6 %all-to-all-start = ((bf16[32,256,128]{2,1,0:T(8,128)(2,1)}), bf16[32,256,128]{2,1,0:T(8,128)(2,1)S(1)}, u32[]{:S(2)}, u32[]{:S(2)}) async-start(bf16[32,256,128]{2,1,0:T(8,128)(2,1)} %meet.1), calls=%async_computation | async-start | bytes 4194304 | tf_op jit(solution)/shard_map/all_to_all | solution.py:470
  68.8 15.7 %collective-permute-start.3 = (bf16[32,64,128]{2,1,0:T(8,128)(2,1)S(1)}, bf16[32,64,128]{2,1,0:T(8,128)(2,1)S(1)}, u32[]{:S(2)}, u32[]{:S(2)}) collective-permute-start(bf16[32,64,128]{2,1,0:T(8,128)(2,1)S(1)} %slice.4), channel_id=1, source_target_pairs={{0,64},{1,65},{64,0},{65,1},{2,66},{3,67},{66,2},{67,3},{4,68},{5,... | collective-permute-start | bytes 1572872 | tf_op jit(solution)/shard_map/ppermute | solution.py:462
  86.1 1.0 copy-start.1
  96.0 1.2 copy-start.2
  122.1 7.4 %collective-permute-start.4 = (bf16[2,16,640]{2,1,0:T(8,128)(2,1)S(1)}, bf16[2,16,640]{2,1,0:T(8,128)(2,1)S(1)}, u32[]{:S(2)}, u32[]{:S(2)}) collective-permute-start(bf16[2,16,640]{2,1,0:T(8,128)(2,1)S(1)} %get-tuple-element.19), channel_id=1, source_target_pairs={{0,8},{8,16},{16,24},{24,32},{32,40},{40,48},{48,56},{56,64},{64,7... | collective-permute-start | bytes 122888 | tf_op jit(solution)/shard_map/ppermute | solution.py:453
  122.1 7.3 %collective-permute-start.5 = (bf16[2,16,640]{2,1,0:T(8,128)(2,1)S(1)}, bf16[2,16,640]{2,1,0:T(8,128)(2,1)S(1)}, u32[]{:S(2)}, u32[]{:S(2)}) collective-permute-start(bf16[2,16,640]{2,1,0:T(8,128)(2,1)S(1)} %get-tuple-element.20), channel_id=1, source_target_pairs={{0,120},{8,0},{16,8},{24,16},{32,24},{40,32},{48,40},{56,48},{64,5... | collective-permute-start | bytes 122888 | tf_op jit(solution)/shard_map/ppermute | solution.py:453

commit v2 on v1

--- a/solution.py
+++ b/solution.py
@@ -22,9 +22,8 @@
 
 
 def split_bf16(table):
-    high = table.astype(jnp.bfloat16)
-    low = (table - high.astype(jnp.float32)).astype(jnp.bfloat16)
-    return jnp.concatenate([high, low], axis=0)
+    high = lax.reduce_precision(table, exponent_bits=8, mantissa_bits=7)
+    return jnp.concatenate([high, table - high], axis=0).astype(jnp.bfloat16)
 
 
 def tables():

time: 136 us -> 136 us (level)
  no operation moved by 1% of the time
where the time goes in v2:
time: 136 us; the launch traced here: 134 us
  waiting for transfers between devices  50 us (37%)
  starting transfers between devices  29 us (21%)
  Pallas kernels  28.1 us (21%)
  blocking collectives  21.6 us (16%)
  local copies, waits for them, and re-layouts  4.12 us (3%)
    ppermute x4, waiting for transfers between devices, between_y(): return lax.ppermute(value, ('yh', 'gz'), pairs)  40.9 us
    all_to_all x1, blocking collectives, exchanged(): return lax.all_to_all(array, axes, split_axis=0, concat_axis=0, tiled=True)  21.6 us
    all_to_all x2, starting transfers between devices, exchanged(): return lax.all_to_all(array, axes, split_axis=0, concat_axis=0, tiled=True)  16.3 us
    pallas_call x3, Pallas kernels, x_transform(): pl.pallas_call(lambda *refs: x_kernel(fields, rows_local, *refs), grid=(r...  14 us
    all_to_all x2, waiting for transfers between devices, exchanged(): return lax.all_to_all(array, axes, split_axis=0, concat_axis=0, tiled=True)  9.01 us
    ppermute x4, starting transfers between devices, between_y(): return lax.ppermute(value, ('yh', 'gz'), pairs)  7.22 us
    ppermute x2, starting transfers between devices, ring(): lax.ppermute(value, axis, [(i, (i + steps) % count) for i in range(count)])  5.42 us
    pallas_call x2, Pallas kernels, y_transform(): pl.pallas_call(kernel, out_shape=jax.ShapeDtypeStruct((8, 32, 2304), jnp....  4.68 us
  transfers between devices with their start and end apart: 8, of which 4 were waited for; matrix products, arithmetic and copies ran while one was open for 0% of the time, Pallas kernels for 11%

profile of v2, /device:TPU:0, one launch (start us, length us, event | category | flops | bytes accessed | tf_op | source)
XLA Modules:
  0.0 134.0 jit_solution(10930784763381990331)
XLA Ops:
  0.0 0.1 fusion.41
  0.1 0.3 fusion.39
  0.5 0.0 copy-start
  0.5 1.9 %copy-done = bf16[3,2,1,64,4096]{4,3,2,1,0:T(8,128)(2,1)S(1)} copy-done((bf16[3,2,1,64,4096]{4,3,2,1,0:T(8,128)(2,1)S(1)}, bf16[3,2,1,64,4096]{4,3,2,1,0:T(8,128)(2,1)}, u32[]{:S(2)}) %copy-start) | copy-done | bytes 3145752
  2.4 5.4 %lines_curl_x_curl_y.1 = (bf16[32,128,128]{2,1,0:T(8,128)(2,1)S(1)}, bf16[32,128,128]{2,1,0:T(8,128)(2,1)}) custom-call(bf16[3,2,64,4096]{3,2,1,0:T(8,128)(2,1)S(1)} %bitcast.1, bf16[3,2,64,4096]{3,2,1,0:T(8,128)(2,1)S(1)} %bitcast.2, bf16[3,2,64,4096]{3,2,1,0:T(8,128)(2,1)S(1)} %bitcast.3, bf16[512,256]{1,0:T(8,128)(2,1)S(1)} %pad_maximum_fusion.refs_3_.refs_2_, ...), custom_call_target="tpu_custom_call" | custom-call | flops 1073741824 | bytes 4194304 | tf_op jit(solution)/shard_map/lines_curl_x_curl_y/pallas_call | solution.py:177
  7.8 3.3 %collective-permute-start = (bf16[32,128,128]{2,1,0:T(8,128)(2,1)}, bf16[32,128,128]{2,1,0:T(8,128)(2,1)S(1)}, u32[]{:S(2)}, u32[]{:S(2)}) collective-permute-start(bf16[32,128,128]{2,1,0:T(8,128)(2,1)} %get-tuple-element.14), channel_id=1, source_target_pairs={{0,64},{1,65},{64,0},{65,1},{2,66},{3,67},{66,2},{67,3},{4,68},{5,... | collective-permute-start | bytes 3145736 | tf_op jit(solution)/shard_map/ppermute | solution.py:461
  11.1 3.5 %lines_curl_z.1.refs_4_ = bf16[32,128,128]{2,1,0:T(8,128)(2,1)} custom-call(bf16[3,2,64,4096]{3,2,1,0:T(8,128)(2,1)S(1)} %bitcast.4, bf16[3,2,64,4096]{3,2,1,0:T(8,128)(2,1)S(1)} %bitcast.5, bf16[512,256]{1,0:T(8,128)(2,1)S(1)} %pad_maximum_fusion.refs_3_.refs_2_, f32[2,32,128]{2,1,0:T(8,128)S(1)} %maximum_multiply_fusion.1.refs_4_.refs_3_, ...), custom_call_target="tpu_custom_call" | custom-call | flops 1073741824 | bytes 4194304 | tf_op jit(solution)/shard_map/lines_curl_z/pallas_call | solution.py:177
  14.6 5.1 %lines_u_v.1 = (bf16[32,128,128]{2,1,0:T(8,128)(2,1)}, bf16[32,128,128]{2,1,0:T(8,128)(2,1)}) custom-call(bf16[3,2,64,4096]{3,2,1,0:T(8,128)(2,1)S(1)} %bitcast.6, bf16[3,2,64,4096]{3,2,1,0:T(8,128)(2,1)S(1)} %bitcast.7, bf16[512,256]{1,0:T(8,128)(2,1)S(1)} %pad_maximum_fusion.refs_3_.refs_2_, f32[2,32,128]{2,1,0:T(8,128)S(1)} %maximum_multiply_fusion.1.refs_4_.refs_3_, ...), custom_call_target="tpu_custom_call" | custom-call | flops 1073741824 | bytes 4194304 | tf_op jit(solution)/shard_map/lines_u_v/pallas_call | solution.py:177
  19.7 0.7 collective-permute-start.1
  20.4 0.4 collective-permute-start.2
  20.8 8.2 %all-to-all-start.1 = ((bf16[32,128,128]{2,1,0:T(8,128)(2,1)}), bf16[32,128,128]{2,1,0:T(8,128)(2,1)S(1)}, u32[]{:S(2)}, u32[]{:S(2)}) async-start(bf16[32,128,128]{2,1,0:T(8,128)(2,1)} %lines_curl_z.1.refs_4_), calls=%async_computation.1 | async-start | bytes 2097152 | tf_op jit(solution)/shard_map/all_to_all | solution.py:469
  28.9 6.7 %collective-permute-done.came = bf16[32,128,128]{2,1,0:T(8,128)(2,1)S(1)} collective-permute-done((bf16[32,128,128]{2,1,0:T(8,128)(2,1)}, bf16[32,128,128]{2,1,0:T(8,128)(2,1)S(1)}, u32[]{:S(2)}, u32[]{:S(2)}) %collective-permute-start) | collective-permute-done | bytes 1048608 | tf_op jit(solution)/shard_map/ppermute | solution.py:461
  35.6 21.9 %collective-permute-done.1.near = bf16[32,128,128]{2,1,0:T(8,128)(2,1)} collective-permute-done((bf16[32,128,128]{2,1,0:T(8,128)(2,1)}, bf16[32,128,128]{2,1,0:T(8,128)(2,1)}, u32[]{:S(2)}, u32[]{:S(2)}) %collective-permute-start.1) | collective-permute-done | bytes 1048608 | tf_op jit(solution)/shard_map/ppermute | solution.py:461
  57.5 2.8 %meet.1 = bf16[32,256,128]{2,1,0:T(8,128)(2,1)} custom-call(bf16[32,128,128]{2,1,0:T(8,128)(2,1)S(1)} %get-tuple-element.13.refs_4_.own, bf16[32,128,128]{2,1,0:T(8,128)(2,1)S(1)} %collective-permute-done.came, bf16[32,128,128]{2,1,0:T(8,128)(2,1)} %collective-permute-done.1.near, bf16[32,128,128]{2,1,0:T(8,128)(2,1)} %collective-permute-done.2.across), custom_call_target="tpu_custom_call" | custom-call | flops 1048576 | bytes 4194304 | tf_op jit(solution)/shard_map/meet/pallas_call | solution.py:205
  60.3 8.2 %all-to-all-start = ((bf16[32,256,128]{2,1,0:T(8,128)(2,1)}), bf16[32,256,128]{2,1,0:T(8,128)(2,1)S(1)}, u32[]{:S(2)}, u32[]{:S(2)}) async-start(bf16[32,256,128]{2,1,0:T(8,128)(2,1)} %meet.1), calls=%async_computation | async-start | bytes 4194304 | tf_op jit(solution)/shard_map/all_to_all | solution.py:469
  68.5 0.1 sine_negate_fusion
  68.7 2.9 %collective-permute-start.3 = (bf16[32,64,128]{2,1,0:T(8,128)(2,1)S(1)}, bf16[32,64,128]{2,1,0:T(8,128)(2,1)S(1)}, u32[]{:S(2)}, u32[]{:S(2)}) collective-permute-start(bf16[32,64,128]{2,1,0:T(8,128)(2,1)S(1)} %slice.4), channel_id=1, source_target_pairs={{0,64},{1,65},{64,0},{65,1},{2,66},{3,67},{66,2},{67,3},{4,68},{5,... | collective-permute-start | bytes 1572872 | tf_op jit(solution)/shard_map/ppermute | solution.py:461
  71.6 0.1 fusion.29
  71.7 0.1 pad_maximum_fusion.2.twist
  71.8 0.1 reduce-precision_convert_fusion.1
  72.0 12.4 %collective-permute-done.3.came = bf16[32,64,128]{2,1,0:T(8,128)(2,1)S(1)} collective-permute-done((bf16[32,64,128]{2,1,0:T(8,128)(2,1)S(1)}, bf16[32,64,128]{2,1,0:T(8,128)(2,1)S(1)}, u32[]{:S(2)}, u32[]{:S(2)}) %collective-permute-start.3) | collective-permute-done | bytes 524320 | tf_op jit(solution)/shard_map/ppermute | solution.py:461
  84.4 1.6 %y_first.1.before = f32[128,2048]{1,0:T(8,128)S(1)} custom-call(bf16[32,128,128]{2,1,0:T(8,128)(2,1)S(1)} %all-to-all-done.1.own, bf16[32,64,128]{2,1,0:T(8,128)(2,1)S(1)} %collective-permute-done.3.came, bf16[256,256]{1,0:T(8,128)(2,1)S(1)} %pad_maximum_fusion.1.matrix, f32[2,64,128]{2,1,0:T(8,128)S(1)} %pad_maximum_fusion.2.twist), custom_call_target="tpu_custom_call" | custom-call | flops 268435456 | bytes 4194304 | tf_op jit(solution)/shard_map/y_first/pallas_call | solution.py:286
  86.0 1.0 copy-done.1
  86.9 9.0 %all-to-all-done.source = bf16[32,256,128]{2,1,0:T(8,128)(2,1)S(1)} async-done(((bf16[32,256,128]{2,1,0:T(8,128)(2,1)}), bf16[32,256,128]{2,1,0:T(8,128)(2,1)S(1)}, u32[]{:S(2)}, u32[]{:S(2)}) %all-to-all-start) | async-done | bytes 2097184 | tf_op jit(solution)/shard_map/all_to_all | solution.py:469
  96.0 1.2 copy-done.2
  97.2 3.1 %y_last.1 = bf16[8,32,2304]{2,1,0:T(8,128)(2,1)S(1)} custom-call(bf16[32,256,128]{2,1,0:T(8,128)(2,1)S(1)} %all-to-all-done.source, f32[128,2048]{1,0:T(8,128)S(1)} %copy-done.2, bf16[256,256]{1,0:T(8,128)(2,1)S(1)} %pad_maximum_fusion.1.matrix, f32[2,64,128]{2,1,0:T(8,128)S(1)} %pad_maximum_fusion.2.twist), custom_call_target="tpu_custom_call" | custom-call | flops 268435456 | bytes 4194304 | tf_op jit(solution)/shard_map/y_last/pallas_call | solution.py:286
  100.3 21.6 %all_to_all.15.field = bf16[8,32,2304]{2,1,0:T(8,128)(2,1)S(1)} all-to-all(bf16[8,32,2304]{2,1,0:T(8,128)(2,1)S(1)} %y_last.1), channel_id=1, replica_groups=mesh['yh'=2,'zc'=8,'col'=4,'gz'=2] {'gz','col'}, dimensions={0} | all-to-all | bytes 2359296 | tf_op jit(solution)/shard_map/all_to_all | solution.py:469
  121.9 0.1 edges.1
  122.0 0.1 collective-permute-start.4
  122.1 5.3 %collective-permute-start.5 = (bf16[2,16,640]{2,1,0:T(8,128)(2,1)S(1)}, bf16[2,16,640]{2,1,0:T(8,128)(2,1)S(1)}, u32[]{:S(2)}, u32[]{:S(2)}) collective-permute-start(bf16[2,16,640]{2,1,0:T(8,128)(2,1)S(1)} %get-tuple-element.20), channel_id=1, source_target_pairs={{0,120},{8,0},{16,8},{24,16},{32,24},{40,32},{48,40},{56,48},{64,5... | collective-permute-start | bytes 122888 | tf_op jit(solution)/shard_map/ppermute | solution.py:452
  127.5 2.0 %regroup.1 = (f32[72,16,256]{2,1,0:T(8,128)S(1)}, f32[72,16,256]{2,1,0:T(8,128)S(1)}) custom-call(bf16[8,32,2304]{2,1,0:T(8,128)(2,1)S(1)} %all_to_all.15.field), custom_call_target="tpu_custom_call" | custom-call | flops 16777216 | bytes 8388608 | tf_op jit(solution)/shard_map/regroup/pallas_call | solution.py:341
  129.5 4.5 %smooth.1 = f32[1,1024,256]{2,1,0:T(8,128)} custom-call(f32[72,16,256]{2,1,0:T(8,128)S(1)} %get-tuple-element.17.own, f32[72,16,256]{2,1,0:T(8,128)S(1)} %get-tuple-element.18.other, bf16[2,16,640]{2,1,0:T(8,128)(2,1)S(1)} %collective-permute-done.4.low, bf16[2,16,640]{2,1,0:T(8,128)(2,1)S(1)} %collective-permute-done.5.high), custom_call_target="tpu_custom_call" | custom-call | tf_op jit(solution)/shard_map/smooth/pallas_call | solution.py:436
  (15 shorter events, 0.1 us)
Async XLA Ops:
  0.5 1.9 %copy-start = (bf16[3,2,1,64,4096]{4,3,2,1,0:T(8,128)(2,1)S(1)}, bf16[3,2,1,64,4096]{4,3,2,1,0:T(8,128)(2,1)}, u32[]{:S(2)}) copy-start(bf16[3,2,1,64,4096]{4,3,2,1,0:T(8,128)(2,1)} %param.1) | copy-start | bytes 9437188
  7.8 27.8 %collective-permute-start = (bf16[32,128,128]{2,1,0:T(8,128)(2,1)}, bf16[32,128,128]{2,1,0:T(8,128)(2,1)S(1)}, u32[]{:S(2)}, u32[]{:S(2)}) collective-permute-start(bf16[32,128,128]{2,1,0:T(8,128)(2,1)} %get-tuple-element.14), channel_id=1, source_target_pairs={{0,64},{1,65},{64,0},{65,1},{2,66},{3,67},{66,2},{67,3},{4,68},{5,... | collective-permute-start | bytes 3145736 | tf_op jit(solution)/shard_map/ppermute | solution.py:461
  19.7 37.8 %collective-permute-start.1 = (bf16[32,128,128]{2,1,0:T(8,128)(2,1)}, bf16[32,128,128]{2,1,0:T(8,128)(2,1)}, u32[]{:S(2)}, u32[]{:S(2)}) collective-permute-start(bf16[32,128,128]{2,1,0:T(8,128)(2,1)} %get-tuple-element.15), channel_id=1, source_target_pairs={{0,1},{1,0},{64,65},{65,64},{2,3},{3,2},{66,67},{67,66},{4,5},{5,4... | collective-permute-start | bytes 3145736 | tf_op jit(solution)/shard_map/ppermute | solution.py:461
  20.4 37.1 %collective-permute-start.2 = (bf16[32,128,128]{2,1,0:T(8,128)(2,1)}, bf16[32,128,128]{2,1,0:T(8,128)(2,1)}, u32[]{:S(2)}, u32[]{:S(2)}) collective-permute-start(bf16[32,128,128]{2,1,0:T(8,128)(2,1)} %get-tuple-element.16), channel_id=1, source_target_pairs={{0,65},{1,64},{64,1},{65,0},{2,67},{3,66},{66,3},{67,2},{4,69},{5,... | collective-permute-start | bytes 3145736 | tf_op jit(solution)/shard_map/ppermute | solution.py:461
  20.8 39.5 %all-to-all-start.1 = ((bf16[32,128,128]{2,1,0:T(8,128)(2,1)}), bf16[32,128,128]{2,1,0:T(8,128)(2,1)S(1)}, u32[]{:S(2)}, u32[]{:S(2)}) async-start(bf16[32,128,128]{2,1,0:T(8,128)(2,1)} %lines_curl_z.1.refs_4_), calls=%async_computation.1 | async-start | bytes 2097152 | tf_op jit(solution)/shard_map/all_to_all | solution.py:469
  60.3 35.6 %all-to-all-start = ((bf16[32,256,128]{2,1,0:T(8,128)(2,1)}), bf16[32,256,128]{2,1,0:T(8,128)(2,1)S(1)}, u32[]{:S(2)}, u32[]{:S(2)}) async-start(bf16[32,256,128]{2,1,0:T(8,128)(2,1)} %meet.1), calls=%async_computation | async-start | bytes 4194304 | tf_op jit(solution)/shard_map/all_to_all | solution.py:469
  68.7 15.7 %collective-permute-start.3 = (bf16[32,64,128]{2,1,0:T(8,128)(2,1)S(1)}, bf16[32,64,128]{2,1,0:T(8,128)(2,1)S(1)}, u32[]{:S(2)}, u32[]{:S(2)}) collective-permute-start(bf16[32,64,128]{2,1,0:T(8,128)(2,1)S(1)} %slice.4), channel_id=1, source_target_pairs={{0,64},{1,65},{64,0},{65,1},{2,66},{3,67},{66,2},{67,3},{4,68},{5,... | collective-permute-start | bytes 1572872 | tf_op jit(solution)/shard_map/ppermute | solution.py:461
  86.0 1.0 copy-start.1
  95.9 1.2 copy-start.2
  122.0 7.4 %collective-permute-start.4 = (bf16[2,16,640]{2,1,0:T(8,128)(2,1)S(1)}, bf16[2,16,640]{2,1,0:T(8,128)(2,1)S(1)}, u32[]{:S(2)}, u32[]{:S(2)}) collective-permute-start(bf16[2,16,640]{2,1,0:T(8,128)(2,1)S(1)} %get-tuple-element.19), channel_id=1, source_target_pairs={{0,8},{8,16},{16,24},{24,32},{32,40},{40,48},{48,56},{56,64},{64,7... | collective-permute-start | bytes 122888 | tf_op jit(solution)/shard_map/ppermute | solution.py:452
  122.1 7.3 %collective-permute-start.5 = (bf16[2,16,640]{2,1,0:T(8,128)(2,1)S(1)}, bf16[2,16,640]{2,1,0:T(8,128)(2,1)S(1)}, u32[]{:S(2)}, u32[]{:S(2)}) collective-permute-start(bf16[2,16,640]{2,1,0:T(8,128)(2,1)S(1)} %get-tuple-element.20), channel_id=1, source_target_pairs={{0,120},{8,0},{16,8},{24,16},{32,24},{40,32},{48,40},{56,48},{64,5... | collective-permute-start | bytes 122888 | tf_op jit(solution)/shard_map/ppermute | solution.py:452

commit v3 on v2

--- a/solution.py
+++ b/solution.py
@@ -183,7 +183,7 @@
         scratch_shapes=[
             pltpu.VMEM((2, 32, 16, 128), jnp.float32),
             pltpu.VMEM((len(fields), 2048, 256), jnp.bfloat16),
-            pltpu.VMEM((64 * PAD, 128), jnp.float32),
+            pltpu.VMEM((65 * PAD, 128), jnp.float32),
         ],
         compiler_params=pltpu.CompilerParams(vmem_limit_bytes=VMEM_LIMIT),
         cost_estimate=pl.CostEstimate(flops=2**30, bytes_accessed=2**22, transcendentals=0),
@@ -440,7 +440,7 @@
             pltpu.VMEM((72, 16, 128), jnp.float32),
             pltpu.VMEM((72, 16, 128), jnp.float32),
             pltpu.VMEM((2, 72, 16, 384), jnp.float32),
-            pltpu.VMEM((32 * PAD, 128), jnp.float32),
+            pltpu.VMEM((33 * PAD, 128), jnp.float32),
         ],
         compiler_params=pltpu.CompilerParams(vmem_limit_bytes=VMEM_LIMIT),
         name="smooth",

time: 136 us -> 136 us (level)
  no operation moved by 1% of the time
where the time goes in v3:
time: 136 us; the launch traced here: 134 us
  waiting for transfers between devices  50 us (37%)
  starting transfers between devices  29 us (21%)
  Pallas kernels  28.1 us (21%)
  blocking collectives  21.6 us (16%)
  local copies, waits for them, and re-layouts  4.12 us (3%)
    ppermute x4, waiting for transfers between devices, between_y(): return lax.ppermute(value, ('yh', 'gz'), pairs)  41 us
    all_to_all x1, blocking collectives, exchanged(): return lax.all_to_all(array, axes, split_axis=0, concat_axis=0, tiled=True)  21.6 us
    all_to_all x2, starting transfers between devices, exchanged(): return lax.all_to_all(array, axes, split_axis=0, concat_axis=0, tiled=True)  16.3 us
    pallas_call x3, Pallas kernels, x_transform(): pl.pallas_call(lambda *refs: x_kernel(fields, rows_local, *refs), grid=(r...  14 us
    all_to_all x2, waiting for transfers between devices, exchanged(): return lax.all_to_all(array, axes, split_axis=0, concat_axis=0, tiled=True)  9.01 us
    ppermute x4, starting transfers between devices, between_y(): return lax.ppermute(value, ('yh', 'gz'), pairs)  7.22 us
    ppermute x2, starting transfers between devices, ring(): lax.ppermute(value, axis, [(i, (i + steps) % count) for i in range(count)])  5.42 us
    pallas_call x2, Pallas kernels, y_transform(): pl.pallas_call(kernel, out_shape=jax.ShapeDtypeStruct((8, 32, 2304), jnp....  4.68 us
  transfers between devices with their start and end apart: 8, of which 4 were waited for; matrix products, arithmetic and copies ran while one was open for 0% of the time, Pallas kernels for 11%

profile of v3, /device:TPU:0, one launch (start us, length us, event | category | flops | bytes accessed | tf_op | source)
XLA Modules:
  0.0 133.9 jit_solution(4049902516588292711)
XLA Ops:
  0.0 0.1 fusion.41
  0.1 0.3 fusion.39
  0.5 0.0 copy-start
  0.5 1.9 %copy-done = bf16[3,2,1,64,4096]{4,3,2,1,0:T(8,128)(2,1)S(1)} copy-done((bf16[3,2,1,64,4096]{4,3,2,1,0:T(8,128)(2,1)S(1)}, bf16[3,2,1,64,4096]{4,3,2,1,0:T(8,128)(2,1)}, u32[]{:S(2)}) %copy-start) | copy-done | bytes 3145752
  2.4 5.4 %lines_curl_x_curl_y.1 = (bf16[32,128,128]{2,1,0:T(8,128)(2,1)S(1)}, bf16[32,128,128]{2,1,0:T(8,128)(2,1)}) custom-call(bf16[3,2,64,4096]{3,2,1,0:T(8,128)(2,1)S(1)} %bitcast.1, bf16[3,2,64,4096]{3,2,1,0:T(8,128)(2,1)S(1)} %bitcast.2, bf16[3,2,64,4096]{3,2,1,0:T(8,128)(2,1)S(1)} %bitcast.3, bf16[512,256]{1,0:T(8,128)(2,1)S(1)} %pad_maximum_fusion.refs_3_.refs_2_, ...), custom_call_target="tpu_custom_call" | custom-call | flops 1073741824 | bytes 4194304 | tf_op jit(solution)/shard_map/lines_curl_x_curl_y/pallas_call | solution.py:177
  7.8 3.3 %collective-permute-start = (bf16[32,128,128]{2,1,0:T(8,128)(2,1)}, bf16[32,128,128]{2,1,0:T(8,128)(2,1)S(1)}, u32[]{:S(2)}, u32[]{:S(2)}) collective-permute-start(bf16[32,128,128]{2,1,0:T(8,128)(2,1)} %get-tuple-element.14), channel_id=1, source_target_pairs={{0,64},{1,65},{64,0},{65,1},{2,66},{3,67},{66,2},{67,3},{4,68},{5,... | collective-permute-start | bytes 3145736 | tf_op jit(solution)/shard_map/ppermute | solution.py:461
  11.1 3.5 %lines_curl_z.1.refs_4_ = bf16[32,128,128]{2,1,0:T(8,128)(2,1)} custom-call(bf16[3,2,64,4096]{3,2,1,0:T(8,128)(2,1)S(1)} %bitcast.4, bf16[3,2,64,4096]{3,2,1,0:T(8,128)(2,1)S(1)} %bitcast.5, bf16[512,256]{1,0:T(8,128)(2,1)S(1)} %pad_maximum_fusion.refs_3_.refs_2_, f32[2,32,128]{2,1,0:T(8,128)S(1)} %maximum_multiply_fusion.1.refs_4_.refs_3_, ...), custom_call_target="tpu_custom_call" | custom-call | flops 1073741824 | bytes 4194304 | tf_op jit(solution)/shard_map/lines_curl_z/pallas_call | solution.py:177
  14.5 5.1 %lines_u_v.1 = (bf16[32,128,128]{2,1,0:T(8,128)(2,1)}, bf16[32,128,128]{2,1,0:T(8,128)(2,1)}) custom-call(bf16[3,2,64,4096]{3,2,1,0:T(8,128)(2,1)S(1)} %bitcast.6, bf16[3,2,64,4096]{3,2,1,0:T(8,128)(2,1)S(1)} %bitcast.7, bf16[512,256]{1,0:T(8,128)(2,1)S(1)} %pad_maximum_fusion.refs_3_.refs_2_, f32[2,32,128]{2,1,0:T(8,128)S(1)} %maximum_multiply_fusion.1.refs_4_.refs_3_, ...), custom_call_target="tpu_custom_call" | custom-call | flops 1073741824 | bytes 4194304 | tf_op jit(solution)/shard_map/lines_u_v/pallas_call | solution.py:177
  19.7 0.7 collective-permute-start.1
  20.3 0.4 collective-permute-start.2
  20.7 8.2 %all-to-all-start.1 = ((bf16[32,128,128]{2,1,0:T(8,128)(2,1)}), bf16[32,128,128]{2,1,0:T(8,128)(2,1)S(1)}, u32[]{:S(2)}, u32[]{:S(2)}) async-start(bf16[32,128,128]{2,1,0:T(8,128)(2,1)} %lines_curl_z.1.refs_4_), calls=%async_computation.1 | async-start | bytes 2097152 | tf_op jit(solution)/shard_map/all_to_all | solution.py:469
  28.9 6.7 %collective-permute-done.came = bf16[32,128,128]{2,1,0:T(8,128)(2,1)S(1)} collective-permute-done((bf16[32,128,128]{2,1,0:T(8,128)(2,1)}, bf16[32,128,128]{2,1,0:T(8,128)(2,1)S(1)}, u32[]{:S(2)}, u32[]{:S(2)}) %collective-permute-start) | collective-permute-done | bytes 1048608 | tf_op jit(solution)/shard_map/ppermute | solution.py:461
  35.6 21.9 %collective-permute-done.1.near = bf16[32,128,128]{2,1,0:T(8,128)(2,1)} collective-permute-done((bf16[32,128,128]{2,1,0:T(8,128)(2,1)}, bf16[32,128,128]{2,1,0:T(8,128)(2,1)}, u32[]{:S(2)}, u32[]{:S(2)}) %collective-permute-start.1) | collective-permute-done | bytes 1048608 | tf_op jit(solution)/shard_map/ppermute | solution.py:461
  57.4 2.8 %meet.1 = bf16[32,256,128]{2,1,0:T(8,128)(2,1)} custom-call(bf16[32,128,128]{2,1,0:T(8,128)(2,1)S(1)} %get-tuple-element.13.refs_4_.own, bf16[32,128,128]{2,1,0:T(8,128)(2,1)S(1)} %collective-permute-done.came, bf16[32,128,128]{2,1,0:T(8,128)(2,1)} %collective-permute-done.1.near, bf16[32,128,128]{2,1,0:T(8,128)(2,1)} %collective-permute-done.2.across), custom_call_target="tpu_custom_call" | custom-call | flops 1048576 | bytes 4194304 | tf_op jit(solution)/shard_map/meet/pallas_call | solution.py:205
  60.3 8.2 %all-to-all-start = ((bf16[32,256,128]{2,1,0:T(8,128)(2,1)}), bf16[32,256,128]{2,1,0:T(8,128)(2,1)S(1)}, u32[]{:S(2)}, u32[]{:S(2)}) async-start(bf16[32,256,128]{2,1,0:T(8,128)(2,1)} %meet.1), calls=%async_computation | async-start | bytes 4194304 | tf_op jit(solution)/shard_map/all_to_all | solution.py:469
  68.4 0.1 sine_negate_fusion
  68.6 2.9 %collective-permute-start.3 = (bf16[32,64,128]{2,1,0:T(8,128)(2,1)S(1)}, bf16[32,64,128]{2,1,0:T(8,128)(2,1)S(1)}, u32[]{:S(2)}, u32[]{:S(2)}) collective-permute-start(bf16[32,64,128]{2,1,0:T(8,128)(2,1)S(1)} %slice.4), channel_id=1, source_target_pairs={{0,64},{1,65},{64,0},{65,1},{2,66},{3,67},{66,2},{67,3},{4,68},{5,... | collective-permute-start | bytes 1572872 | tf_op jit(solution)/shard_map/ppermute | solution.py:461
  71.5 0.1 fusion.29
  71.7 0.1 pad_maximum_fusion.2.twist
  71.8 0.1 reduce-precision_convert_fusion.1
  71.9 12.4 %collective-permute-done.3.came = bf16[32,64,128]{2,1,0:T(8,128)(2,1)S(1)} collective-permute-done((bf16[32,64,128]{2,1,0:T(8,128)(2,1)S(1)}, bf16[32,64,128]{2,1,0:T(8,128)(2,1)S(1)}, u32[]{:S(2)}, u32[]{:S(2)}) %collective-permute-start.3) | collective-permute-done | bytes 524320 | tf_op jit(solution)/shard_map/ppermute | solution.py:461
  84.3 1.6 %y_first.1.before = f32[128,2048]{1,0:T(8,128)S(1)} custom-call(bf16[32,128,128]{2,1,0:T(8,128)(2,1)S(1)} %all-to-all-done.1.own, bf16[32,64,128]{2,1,0:T(8,128)(2,1)S(1)} %collective-permute-done.3.came, bf16[256,256]{1,0:T(8,128)(2,1)S(1)} %pad_maximum_fusion.1.matrix, f32[2,64,128]{2,1,0:T(8,128)S(1)} %pad_maximum_fusion.2.twist), custom_call_target="tpu_custom_call" | custom-call | flops 268435456 | bytes 4194304 | tf_op jit(solution)/shard_map/y_first/pallas_call | solution.py:286
  85.9 1.0 copy-done.1
  86.9 9.0 %all-to-all-done.source = bf16[32,256,128]{2,1,0:T(8,128)(2,1)S(1)} async-done(((bf16[32,256,128]{2,1,0:T(8,128)(2,1)}), bf16[32,256,128]{2,1,0:T(8,128)(2,1)S(1)}, u32[]{:S(2)}, u32[]{:S(2)}) %all-to-all-start) | async-done | bytes 2097184 | tf_op jit(solution)/shard_map/all_to_all | solution.py:469
  95.9 1.2 copy-done.2
  97.1 3.1 %y_last.1 = bf16[8,32,2304]{2,1,0:T(8,128)(2,1)S(1)} custom-call(bf16[32,256,128]{2,1,0:T(8,128)(2,1)S(1)} %all-to-all-done.source, f32[128,2048]{1,0:T(8,128)S(1)} %copy-done.2, bf16[256,256]{1,0:T(8,128)(2,1)S(1)} %pad_maximum_fusion.1.matrix, f32[2,64,128]{2,1,0:T(8,128)S(1)} %pad_maximum_fusion.2.twist), custom_call_target="tpu_custom_call" | custom-call | flops 268435456 | bytes 4194304 | tf_op jit(solution)/shard_map/y_last/pallas_call | solution.py:286
  100.2 21.6 %all_to_all.15.field = bf16[8,32,2304]{2,1,0:T(8,128)(2,1)S(1)} all-to-all(bf16[8,32,2304]{2,1,0:T(8,128)(2,1)S(1)} %y_last.1), channel_id=1, replica_groups=mesh['yh'=2,'zc'=8,'col'=4,'gz'=2] {'gz','col'}, dimensions={0} | all-to-all | bytes 2359296 | tf_op jit(solution)/shard_map/all_to_all | solution.py:469
  121.8 0.1 edges.1
  122.0 0.1 collective-permute-start.4
  122.1 5.3 %collective-permute-start.5 = (bf16[2,16,640]{2,1,0:T(8,128)(2,1)S(1)}, bf16[2,16,640]{2,1,0:T(8,128)(2,1)S(1)}, u32[]{:S(2)}, u32[]{:S(2)}) collective-permute-start(bf16[2,16,640]{2,1,0:T(8,128)(2,1)S(1)} %get-tuple-element.20), channel_id=1, source_target_pairs={{0,120},{8,0},{16,8},{24,16},{32,24},{40,32},{48,40},{56,48},{64,5... | collective-permute-start | bytes 122888 | tf_op jit(solution)/shard_map/ppermute | solution.py:452
  127.4 2.0 %regroup.1 = (f32[72,16,256]{2,1,0:T(8,128)S(1)}, f32[72,16,256]{2,1,0:T(8,128)S(1)}) custom-call(bf16[8,32,2304]{2,1,0:T(8,128)(2,1)S(1)} %all_to_all.15.field), custom_call_target="tpu_custom_call" | custom-call | flops 16777216 | bytes 8388608 | tf_op jit(solution)/shard_map/regroup/pallas_call | solution.py:341
  129.4 4.5 %smooth.1 = f32[1,1024,256]{2,1,0:T(8,128)} custom-call(f32[72,16,256]{2,1,0:T(8,128)S(1)} %get-tuple-element.17.own, f32[72,16,256]{2,1,0:T(8,128)S(1)} %get-tuple-element.18.other, bf16[2,16,640]{2,1,0:T(8,128)(2,1)S(1)} %collective-permute-done.4.low, bf16[2,16,640]{2,1,0:T(8,128)(2,1)S(1)} %collective-permute-done.5.high), custom_call_target="tpu_custom_call" | custom-call | tf_op jit(solution)/shard_map/smooth/pallas_call | solution.py:436
  (15 shorter events, 0.1 us)
Async XLA Ops:
  0.5 1.9 %copy-start = (bf16[3,2,1,64,4096]{4,3,2,1,0:T(8,128)(2,1)S(1)}, bf16[3,2,1,64,4096]{4,3,2,1,0:T(8,128)(2,1)}, u32[]{:S(2)}) copy-start(bf16[3,2,1,64,4096]{4,3,2,1,0:T(8,128)(2,1)} %param.1) | copy-start | bytes 9437188
  7.8 27.8 %collective-permute-start = (bf16[32,128,128]{2,1,0:T(8,128)(2,1)}, bf16[32,128,128]{2,1,0:T(8,128)(2,1)S(1)}, u32[]{:S(2)}, u32[]{:S(2)}) collective-permute-start(bf16[32,128,128]{2,1,0:T(8,128)(2,1)} %get-tuple-element.14), channel_id=1, source_target_pairs={{0,64},{1,65},{64,0},{65,1},{2,66},{3,67},{66,2},{67,3},{4,68},{5,... | collective-permute-start | bytes 3145736 | tf_op jit(solution)/shard_map/ppermute | solution.py:461
  19.7 37.8 %collective-permute-start.1 = (bf16[32,128,128]{2,1,0:T(8,128)(2,1)}, bf16[32,128,128]{2,1,0:T(8,128)(2,1)}, u32[]{:S(2)}, u32[]{:S(2)}) collective-permute-start(bf16[32,128,128]{2,1,0:T(8,128)(2,1)} %get-tuple-element.15), channel_id=1, source_target_pairs={{0,1},{1,0},{64,65},{65,64},{2,3},{3,2},{66,67},{67,66},{4,5},{5,4... | collective-permute-start | bytes 3145736 | tf_op jit(solution)/shard_map/ppermute | solution.py:461
  20.3 37.1 %collective-permute-start.2 = (bf16[32,128,128]{2,1,0:T(8,128)(2,1)}, bf16[32,128,128]{2,1,0:T(8,128)(2,1)}, u32[]{:S(2)}, u32[]{:S(2)}) collective-permute-start(bf16[32,128,128]{2,1,0:T(8,128)(2,1)} %get-tuple-element.16), channel_id=1, source_target_pairs={{0,65},{1,64},{64,1},{65,0},{2,67},{3,66},{66,3},{67,2},{4,69},{5,... | collective-permute-start | bytes 3145736 | tf_op jit(solution)/shard_map/ppermute | solution.py:461
  20.7 39.5 %all-to-all-start.1 = ((bf16[32,128,128]{2,1,0:T(8,128)(2,1)}), bf16[32,128,128]{2,1,0:T(8,128)(2,1)S(1)}, u32[]{:S(2)}, u32[]{:S(2)}) async-start(bf16[32,128,128]{2,1,0:T(8,128)(2,1)} %lines_curl_z.1.refs_4_), calls=%async_computation.1 | async-start | bytes 2097152 | tf_op jit(solution)/shard_map/all_to_all | solution.py:469
  60.3 35.6 %all-to-all-start = ((bf16[32,256,128]{2,1,0:T(8,128)(2,1)}), bf16[32,256,128]{2,1,0:T(8,128)(2,1)S(1)}, u32[]{:S(2)}, u32[]{:S(2)}) async-start(bf16[32,256,128]{2,1,0:T(8,128)(2,1)} %meet.1), calls=%async_computation | async-start | bytes 4194304 | tf_op jit(solution)/shard_map/all_to_all | solution.py:469
  68.6 15.7 %collective-permute-start.3 = (bf16[32,64,128]{2,1,0:T(8,128)(2,1)S(1)}, bf16[32,64,128]{2,1,0:T(8,128)(2,1)S(1)}, u32[]{:S(2)}, u32[]{:S(2)}) collective-permute-start(bf16[32,64,128]{2,1,0:T(8,128)(2,1)S(1)} %slice.4), channel_id=1, source_target_pairs={{0,64},{1,65},{64,0},{65,1},{2,66},{3,67},{66,2},{67,3},{4,68},{5,... | collective-permute-start | bytes 1572872 | tf_op jit(solution)/shard_map/ppermute | solution.py:461
  85.9 1.0 copy-start.1
  95.9 1.2 copy-start.2
  122.0 7.4 %collective-permute-start.4 = (bf16[2,16,640]{2,1,0:T(8,128)(2,1)S(1)}, bf16[2,16,640]{2,1,0:T(8,128)(2,1)S(1)}, u32[]{:S(2)}, u32[]{:S(2)}) collective-permute-start(bf16[2,16,640]{2,1,0:T(8,128)(2,1)S(1)} %get-tuple-element.19), channel_id=1, source_target_pairs={{0,8},{8,16},{16,24},{24,32},{32,40},{40,48},{48,56},{56,64},{64,7... | collective-permute-start | bytes 122888 | tf_op jit(solution)/shard_map/ppermute | solution.py:452
  122.1 7.3 %collective-permute-start.5 = (bf16[2,16,640]{2,1,0:T(8,128)(2,1)S(1)}, bf16[2,16,640]{2,1,0:T(8,128)(2,1)S(1)}, u32[]{:S(2)}, u32[]{:S(2)}) collective-permute-start(bf16[2,16,640]{2,1,0:T(8,128)(2,1)S(1)} %get-tuple-element.20), channel_id=1, source_target_pairs={{0,120},{8,0},{16,8},{24,16},{32,24},{40,32},{48,40},{56,48},{64,5... | collective-permute-start | bytes 122888 | tf_op jit(solution)/shard_map/ppermute | solution.py:452

commit v4 on v3

--- a/solution.py
+++ b/solution.py
@@ -271,12 +271,14 @@
             for z in range(2):
                 out[z * 4 + c, h * 16 : h * 16 + 16, tile * 128 : tile * 128 + 128] = value[c * 16 : c * 16 + 16]
 
+    upper = (lax.broadcasted_iota(jnp.int32, (64, 128), 0) & 15) < 8
     for h in range(2):
         rows = slice(h * 64, h * 64 + 64)
         for tile in range(16):
-            put(h, tile + 1, total[rows, tile * 128 : tile * 128 + 128])
-        put(h, 0, pltpu.roll(total[rows, 15 * 128 : 16 * 128], 1, 0))
-        put(h, 17, pltpu.roll(total[rows, 0:128], 63, 0))
+            put(h, tile, total[rows, tile * 128 : tile * 128 + 128])
+        before_first = pltpu.roll(total[rows, 15 * 128 : 16 * 128], 1, 0)
+        after_last = pltpu.roll(total[rows, 0:128], 63, 0)
+        put(h, 16, jnp.where(upper, before_first, after_last))
 
 
 def y_transform(kernel, sources, y_matrix, y_twist):
@@ -285,7 +287,7 @@
     scratch = [pltpu.VMEM((2, 64, 16, 128), jnp.float32), pltpu.VMEM((2048, 256), jnp.bfloat16)]
     return pl.pallas_call(
         kernel,
-        out_shape=jax.ShapeDtypeStruct((8, 32, 2304), jnp.bfloat16) if last else sums,
+        out_shape=jax.ShapeDtypeStruct((8, 32, 2176), jnp.bfloat16) if last else sums,
         scratch_shapes=scratch + ([pltpu.VMEM((128, 2048), jnp.float32)] if last else []),
         compiler_params=pltpu.CompilerParams(vmem_limit_bytes=VMEM_LIMIT),
         cost_estimate=pl.CostEstimate(flops=2**28, bytes_accessed=2**22, transcendentals=0),
@@ -298,6 +300,19 @@
     even = np.polynomial.polynomial.polypow([1 - 6 * w + 2 * w, w], 3)
     odd = np.polynomial.polynomial.polypow([1 - 6 * w - 2 * w, w], 3)
     return (even + odd) / 2, (even - odd) / 2
+
+
+def brick_tile(field, source, h, tile):
+    def held(index):
+        start = index * 128 if isinstance(index, int) else pl.multiple_of(index * 128, 128)
+        return field[source, h * 16 : h * 16 + 16, pl.ds(start, 128)].astype(jnp.float32)
+
+    row = lax.broadcasted_iota(jnp.int32, (16, 128), 0)
+    if isinstance(tile, int) and tile == 0:
+        return jnp.where(row == 0, held(16), pltpu.roll(held(15), 1, 0))
+    if isinstance(tile, int) and tile == 17:
+        return jnp.where(row == 15, held(16), pltpu.roll(held(0), 15, 0))
+    return held(tile - 1)
 
 
 def regroup_kernel(field, own, other):
@@ -312,10 +327,9 @@
         )
 
     def regroup(z, target, tile):
-        at = pl.ds(pl.multiple_of(tile * 128, 128), 128)
         for ch in range(2):
             v = {
-                (c, h): field[z * 4 + ch * 2 + c, h * 16 : h * 16 + 16, at].astype(jnp.float32)
+                (c, h): brick_tile(field, z * 4 + ch * 2 + c, h, tile)
                 for c in range(2)
                 for h in range(2)
             }
@@ -329,12 +343,15 @@
                 target[tile * 4 + y1 * 2 + 1, :, ch * 128 : ch * 128 + 128] = y01
 
     def both(step, carry):
-        for t in range(3):
-            regroup(me, own, step * 3 + t)
-            regroup(1 - me, other, step * 3 + t)
+        for t in range(2):
+            regroup(me, own, step * 2 + t + 1)
+            regroup(1 - me, other, step * 2 + t + 1)
         return carry
 
-    lax.fori_loop(0, 6, both, 0)
+    lax.fori_loop(0, 8, both, 0)
+    for tile in (0, 17):
+        regroup(me, own, tile)
+        regroup(1 - me, other, tile)
 
 
 def regroup(field):
@@ -353,10 +370,10 @@
         for group in range(5):
             last = first = jnp.zeros((16, 128), jnp.float32)
             for t in range(min(4, 18 - group * 4)):
-                at = slice((group * 4 + t) * 128, (group * 4 + t) * 128 + 128)
+                tile = group * 4 + t
                 here = (lane & 24) == 8 * t
-                last = jnp.where(here, pltpu.roll(field[z * 4 + 3, 16:32, at].astype(jnp.float32), 100 + 8 * t, 1), last)
-                first = jnp.where(here, pltpu.roll(field[z * 4, 0:16, at].astype(jnp.float32), 4 + 8 * t, 1), first)
+                last = jnp.where(here, pltpu.roll(brick_tile(field, z * 4 + 3, 1, tile), 100 + 8 * t, 1), last)
+                first = jnp.where(here, pltpu.roll(brick_tile(field, z * 4, 0, tile), 4 + 8 * t, 1), first)
             low[z, :, group * 128 : group * 128 + 128] = last.astype(jnp.bfloat16)
             high[z, :, group * 128 : group * 128 + 128] = first.astype(jnp.bfloat16)
 

time: 136 us -> 135 us (level)
  no operation moved by 1% of the time
where the time goes in v4:
time: 135 us; the launch traced here: 134 us
  waiting for transfers between devices  50 us (37%)
  starting transfers between devices  29 us (21%)
  Pallas kernels  28.3 us (21%)
  blocking collectives  21.1 us (16%)
  local copies, waits for them, and re-layouts  4.12 us (3%)
    ppermute x4, waiting for transfers between devices, between_y(): return lax.ppermute(value, ('yh', 'gz'), pairs)  41 us
    all_to_all x1, blocking collectives, exchanged(): return lax.all_to_all(array, axes, split_axis=0, concat_axis=0, tiled=True)  21.1 us
    all_to_all x2, starting transfers between devices, exchanged(): return lax.all_to_all(array, axes, split_axis=0, concat_axis=0, tiled=True)  16.3 us
    pallas_call x3, Pallas kernels, x_transform(): pl.pallas_call(lambda *refs: x_kernel(fields, rows_local, *refs), grid=(r...  14 us
    all_to_all x2, waiting for transfers between devices, exchanged(): return lax.all_to_all(array, axes, split_axis=0, concat_axis=0, tiled=True)  9.01 us
    ppermute x4, starting transfers between devices, between_y(): return lax.ppermute(value, ('yh', 'gz'), pairs)  7.22 us
    ppermute x2, starting transfers between devices, ring(): lax.ppermute(value, axis, [(i, (i + steps) % count) for i in range(count)])  5.42 us
    pallas_call x2, Pallas kernels, y_transform(): pl.pallas_call(kernel, out_shape=jax.ShapeDtypeStruct((8, 32, 2176), jnp....  4.68 us
  transfers between devices with their start and end apart: 8, of which 4 were waited for; matrix products, arithmetic and copies ran while one was open for 0% of the time, Pallas kernels for 11%

profile of v4, /device:TPU:0, one launch (start us, length us, event | category | flops | bytes accessed | tf_op | source)
XLA Modules:
  0.0 133.6 jit_solution(5944242985722626986)
XLA Ops:
  0.0 0.1 fusion.41
  0.1 0.3 fusion.39
  0.5 1.9 %copy-done = bf16[3,2,1,64,4096]{4,3,2,1,0:T(8,128)(2,1)S(1)} copy-done((bf16[3,2,1,64,4096]{4,3,2,1,0:T(8,128)(2,1)S(1)}, bf16[3,2,1,64,4096]{4,3,2,1,0:T(8,128)(2,1)}, u32[]{:S(2)}) %copy-start) | copy-done | bytes 3145752
  2.4 5.4 %lines_curl_x_curl_y.1 = (bf16[32,128,128]{2,1,0:T(8,128)(2,1)S(1)}, bf16[32,128,128]{2,1,0:T(8,128)(2,1)}) custom-call(bf16[3,2,64,4096]{3,2,1,0:T(8,128)(2,1)S(1)} %bitcast.1, bf16[3,2,64,4096]{3,2,1,0:T(8,128)(2,1)S(1)} %bitcast.2, bf16[3,2,64,4096]{3,2,1,0:T(8,128)(2,1)S(1)} %bitcast.3, bf16[512,256]{1,0:T(8,128)(2,1)S(1)} %pad_maximum_fusion.refs_3_.refs_2_, ...), custom_call_target="tpu_custom_call" | custom-call | flops 1073741824 | bytes 4194304 | tf_op jit(solution)/shard_map/lines_curl_x_curl_y/pallas_call | solution.py:177
  7.8 3.3 %collective-permute-start = (bf16[32,128,128]{2,1,0:T(8,128)(2,1)}, bf16[32,128,128]{2,1,0:T(8,128)(2,1)S(1)}, u32[]{:S(2)}, u32[]{:S(2)}) collective-permute-start(bf16[32,128,128]{2,1,0:T(8,128)(2,1)} %get-tuple-element.14), channel_id=1, source_target_pairs={{0,64},{1,65},{64,0},{65,1},{2,66},{3,67},{66,2},{67,3},{4,68},{5,... | collective-permute-start | bytes 3145736 | tf_op jit(solution)/shard_map/ppermute | solution.py:478
  11.1 3.5 %lines_curl_z.1.refs_4_ = bf16[32,128,128]{2,1,0:T(8,128)(2,1)} custom-call(bf16[3,2,64,4096]{3,2,1,0:T(8,128)(2,1)S(1)} %bitcast.4, bf16[3,2,64,4096]{3,2,1,0:T(8,128)(2,1)S(1)} %bitcast.5, bf16[512,256]{1,0:T(8,128)(2,1)S(1)} %pad_maximum_fusion.refs_3_.refs_2_, f32[2,32,128]{2,1,0:T(8,128)S(1)} %maximum_multiply_fusion.1.refs_4_.refs_3_, ...), custom_call_target="tpu_custom_call" | custom-call | flops 1073741824 | bytes 4194304 | tf_op jit(solution)/shard_map/lines_curl_z/pallas_call | solution.py:177
  14.5 5.1 %lines_u_v.1 = (bf16[32,128,128]{2,1,0:T(8,128)(2,1)}, bf16[32,128,128]{2,1,0:T(8,128)(2,1)}) custom-call(bf16[3,2,64,4096]{3,2,1,0:T(8,128)(2,1)S(1)} %bitcast.6, bf16[3,2,64,4096]{3,2,1,0:T(8,128)(2,1)S(1)} %bitcast.7, bf16[512,256]{1,0:T(8,128)(2,1)S(1)} %pad_maximum_fusion.refs_3_.refs_2_, f32[2,32,128]{2,1,0:T(8,128)S(1)} %maximum_multiply_fusion.1.refs_4_.refs_3_, ...), custom_call_target="tpu_custom_call" | custom-call | flops 1073741824 | bytes 4194304 | tf_op jit(solution)/shard_map/lines_u_v/pallas_call | solution.py:177
  19.7 0.7 collective-permute-start.1
  20.3 0.4 collective-permute-start.2
  20.7 8.2 %all-to-all-start.1 = ((bf16[32,128,128]{2,1,0:T(8,128)(2,1)}), bf16[32,128,128]{2,1,0:T(8,128)(2,1)S(1)}, u32[]{:S(2)}, u32[]{:S(2)}) async-start(bf16[32,128,128]{2,1,0:T(8,128)(2,1)} %lines_curl_z.1.refs_4_), calls=%async_computation.1 | async-start | bytes 2097152 | tf_op jit(solution)/shard_map/all_to_all | solution.py:486
  28.9 6.7 %collective-permute-done.came = bf16[32,128,128]{2,1,0:T(8,128)(2,1)S(1)} collective-permute-done((bf16[32,128,128]{2,1,0:T(8,128)(2,1)}, bf16[32,128,128]{2,1,0:T(8,128)(2,1)S(1)}, u32[]{:S(2)}, u32[]{:S(2)}) %collective-permute-start) | collective-permute-done | bytes 1048608 | tf_op jit(solution)/shard_map/ppermute | solution.py:478
  35.6 21.9 %collective-permute-done.1.near = bf16[32,128,128]{2,1,0:T(8,128)(2,1)} collective-permute-done((bf16[32,128,128]{2,1,0:T(8,128)(2,1)}, bf16[32,128,128]{2,1,0:T(8,128)(2,1)}, u32[]{:S(2)}, u32[]{:S(2)}) %collective-permute-start.1) | collective-permute-done | bytes 1048608 | tf_op jit(solution)/shard_map/ppermute | solution.py:478
  57.4 2.8 %meet.1 = bf16[32,256,128]{2,1,0:T(8,128)(2,1)} custom-call(bf16[32,128,128]{2,1,0:T(8,128)(2,1)S(1)} %get-tuple-element.13.refs_4_.own, bf16[32,128,128]{2,1,0:T(8,128)(2,1)S(1)} %collective-permute-done.came, bf16[32,128,128]{2,1,0:T(8,128)(2,1)} %collective-permute-done.1.near, bf16[32,128,128]{2,1,0:T(8,128)(2,1)} %collective-permute-done.2.across), custom_call_target="tpu_custom_call" | custom-call | flops 1048576 | bytes 4194304 | tf_op jit(solution)/shard_map/meet/pallas_call | solution.py:205
  60.3 8.2 %all-to-all-start = ((bf16[32,256,128]{2,1,0:T(8,128)(2,1)}), bf16[32,256,128]{2,1,0:T(8,128)(2,1)S(1)}, u32[]{:S(2)}, u32[]{:S(2)}) async-start(bf16[32,256,128]{2,1,0:T(8,128)(2,1)} %meet.1), calls=%async_computation | async-start | bytes 4194304 | tf_op jit(solution)/shard_map/all_to_all | solution.py:486
  68.4 0.1 sine_negate_fusion
  68.6 2.9 %collective-permute-start.3 = (bf16[32,64,128]{2,1,0:T(8,128)(2,1)S(1)}, bf16[32,64,128]{2,1,0:T(8,128)(2,1)S(1)}, u32[]{:S(2)}, u32[]{:S(2)}) collective-permute-start(bf16[32,64,128]{2,1,0:T(8,128)(2,1)S(1)} %slice.4), channel_id=1, source_target_pairs={{0,64},{1,65},{64,0},{65,1},{2,66},{3,67},{66,2},{67,3},{4,68},{5,... | collective-permute-start | bytes 1572872 | tf_op jit(solution)/shard_map/ppermute | solution.py:478
  71.5 0.1 fusion.29
  71.7 0.1 pad_maximum_fusion.2.twist
  71.8 0.1 reduce-precision_convert_fusion.1
  71.9 12.4 %collective-permute-done.3.came = bf16[32,64,128]{2,1,0:T(8,128)(2,1)S(1)} collective-permute-done((bf16[32,64,128]{2,1,0:T(8,128)(2,1)S(1)}, bf16[32,64,128]{2,1,0:T(8,128)(2,1)S(1)}, u32[]{:S(2)}, u32[]{:S(2)}) %collective-permute-start.3) | collective-permute-done | bytes 524320 | tf_op jit(solution)/shard_map/ppermute | solution.py:478
  84.3 1.6 %y_first.1.before = f32[128,2048]{1,0:T(8,128)S(1)} custom-call(bf16[32,128,128]{2,1,0:T(8,128)(2,1)S(1)} %all-to-all-done.1.own, bf16[32,64,128]{2,1,0:T(8,128)(2,1)S(1)} %collective-permute-done.3.came, bf16[256,256]{1,0:T(8,128)(2,1)S(1)} %pad_maximum_fusion.1.matrix, f32[2,64,128]{2,1,0:T(8,128)S(1)} %pad_maximum_fusion.2.twist), custom_call_target="tpu_custom_call" | custom-call | flops 268435456 | bytes 4194304 | tf_op jit(solution)/shard_map/y_first/pallas_call | solution.py:288
  85.9 0.0 copy-start.1
  85.9 1.0 copy-done.1
  86.9 9.0 %all-to-all-done.source = bf16[32,256,128]{2,1,0:T(8,128)(2,1)S(1)} async-done(((bf16[32,256,128]{2,1,0:T(8,128)(2,1)}), bf16[32,256,128]{2,1,0:T(8,128)(2,1)S(1)}, u32[]{:S(2)}, u32[]{:S(2)}) %all-to-all-start) | async-done | bytes 2097184 | tf_op jit(solution)/shard_map/all_to_all | solution.py:486
  95.9 1.2 copy-done.2
  97.1 3.1 %y_last.1 = bf16[8,32,2176]{2,1,0:T(8,128)(2,1)S(1)} custom-call(bf16[32,256,128]{2,1,0:T(8,128)(2,1)S(1)} %all-to-all-done.source, f32[128,2048]{1,0:T(8,128)S(1)} %copy-done.2, bf16[256,256]{1,0:T(8,128)(2,1)S(1)} %pad_maximum_fusion.1.matrix, f32[2,64,128]{2,1,0:T(8,128)S(1)} %pad_maximum_fusion.2.twist), custom_call_target="tpu_custom_call" | custom-call | flops 268435456 | bytes 4194304 | tf_op jit(solution)/shard_map/y_last/pallas_call | solution.py:288
  100.2 21.1 %all_to_all.15.field = bf16[8,32,2176]{2,1,0:T(8,128)(2,1)S(1)} all-to-all(bf16[8,32,2176]{2,1,0:T(8,128)(2,1)S(1)} %y_last.1), channel_id=1, replica_groups=mesh['yh'=2,'zc'=8,'col'=4,'gz'=2] {'gz','col'}, dimensions={0} | all-to-all | bytes 2228224 | tf_op jit(solution)/shard_map/all_to_all | solution.py:486
  121.3 0.1 edges.1
  121.5 0.1 collective-permute-start.4
  121.5 5.3 %collective-permute-start.5 = (bf16[2,16,640]{2,1,0:T(8,128)(2,1)S(1)}, bf16[2,16,640]{2,1,0:T(8,128)(2,1)S(1)}, u32[]{:S(2)}, u32[]{:S(2)}) collective-permute-start(bf16[2,16,640]{2,1,0:T(8,128)(2,1)S(1)} %get-tuple-element.20), channel_id=1, source_target_pairs={{0,120},{8,0},{16,8},{24,16},{32,24},{40,32},{48,40},{56,48},{64,5... | collective-permute-start | bytes 122888 | tf_op jit(solution)/shard_map/ppermute | solution.py:469
  126.9 2.2 %regroup.1 = (f32[72,16,256]{2,1,0:T(8,128)S(1)}, f32[72,16,256]{2,1,0:T(8,128)S(1)}) custom-call(bf16[8,32,2176]{2,1,0:T(8,128)(2,1)S(1)} %all_to_all.15.field), custom_call_target="tpu_custom_call" | custom-call | flops 16777216 | bytes 8388608 | tf_op jit(solution)/shard_map/regroup/pallas_call | solution.py:358
  129.1 4.5 %smooth.1 = f32[1,1024,256]{2,1,0:T(8,128)} custom-call(f32[72,16,256]{2,1,0:T(8,128)S(1)} %get-tuple-element.17.own, f32[72,16,256]{2,1,0:T(8,128)S(1)} %get-tuple-element.18.other, bf16[2,16,640]{2,1,0:T(8,128)(2,1)S(1)} %collective-permute-done.4.low, bf16[2,16,640]{2,1,0:T(8,128)(2,1)S(1)} %collective-permute-done.5.high), custom_call_target="tpu_custom_call" | custom-call | tf_op jit(solution)/shard_map/smooth/pallas_call | solution.py:453
  (15 shorter events, 0.1 us)
Async XLA Ops:
  0.5 1.9 %copy-start = (bf16[3,2,1,64,4096]{4,3,2,1,0:T(8,128)(2,1)S(1)}, bf16[3,2,1,64,4096]{4,3,2,1,0:T(8,128)(2,1)}, u32[]{:S(2)}) copy-start(bf16[3,2,1,64,4096]{4,3,2,1,0:T(8,128)(2,1)} %param.1) | copy-start | bytes 9437188
  7.8 27.8 %collective-permute-start = (bf16[32,128,128]{2,1,0:T(8,128)(2,1)}, bf16[32,128,128]{2,1,0:T(8,128)(2,1)S(1)}, u32[]{:S(2)}, u32[]{:S(2)}) collective-permute-start(bf16[32,128,128]{2,1,0:T(8,128)(2,1)} %get-tuple-element.14), channel_id=1, source_target_pairs={{0,64},{1,65},{64,0},{65,1},{2,66},{3,67},{66,2},{67,3},{4,68},{5,... | collective-permute-start | bytes 3145736 | tf_op jit(solution)/shard_map/ppermute | solution.py:478
  19.7 37.8 %collective-permute-start.1 = (bf16[32,128,128]{2,1,0:T(8,128)(2,1)}, bf16[32,128,128]{2,1,0:T(8,128)(2,1)}, u32[]{:S(2)}, u32[]{:S(2)}) collective-permute-start(bf16[32,128,128]{2,1,0:T(8,128)(2,1)} %get-tuple-element.15), channel_id=1, source_target_pairs={{0,1},{1,0},{64,65},{65,64},{2,3},{3,2},{66,67},{67,66},{4,5},{5,4... | collective-permute-start | bytes 3145736 | tf_op jit(solution)/shard_map/ppermute | solution.py:478
  20.3 37.1 %collective-permute-start.2 = (bf16[32,128,128]{2,1,0:T(8,128)(2,1)}, bf16[32,128,128]{2,1,0:T(8,128)(2,1)}, u32[]{:S(2)}, u32[]{:S(2)}) collective-permute-start(bf16[32,128,128]{2,1,0:T(8,128)(2,1)} %get-tuple-element.16), channel_id=1, source_target_pairs={{0,65},{1,64},{64,1},{65,0},{2,67},{3,66},{66,3},{67,2},{4,69},{5,... | collective-permute-start | bytes 3145736 | tf_op jit(solution)/shard_map/ppermute | solution.py:478
  20.7 39.5 %all-to-all-start.1 = ((bf16[32,128,128]{2,1,0:T(8,128)(2,1)}), bf16[32,128,128]{2,1,0:T(8,128)(2,1)S(1)}, u32[]{:S(2)}, u32[]{:S(2)}) async-start(bf16[32,128,128]{2,1,0:T(8,128)(2,1)} %lines_curl_z.1.refs_4_), calls=%async_computation.1 | async-start | bytes 2097152 | tf_op jit(solution)/shard_map/all_to_all | solution.py:486
  60.3 35.6 %all-to-all-start = ((bf16[32,256,128]{2,1,0:T(8,128)(2,1)}), bf16[32,256,128]{2,1,0:T(8,128)(2,1)S(1)}, u32[]{:S(2)}, u32[]{:S(2)}) async-start(bf16[32,256,128]{2,1,0:T(8,128)(2,1)} %meet.1), calls=%async_computation | async-start | bytes 4194304 | tf_op jit(solution)/shard_map/all_to_all | solution.py:486
  68.6 15.7 %collective-permute-start.3 = (bf16[32,64,128]{2,1,0:T(8,128)(2,1)S(1)}, bf16[32,64,128]{2,1,0:T(8,128)(2,1)S(1)}, u32[]{:S(2)}, u32[]{:S(2)}) collective-permute-start(bf16[32,64,128]{2,1,0:T(8,128)(2,1)S(1)} %slice.4), channel_id=1, source_target_pairs={{0,64},{1,65},{64,0},{65,1},{2,66},{3,67},{66,2},{67,3},{4,68},{5,... | collective-permute-start | bytes 1572872 | tf_op jit(solution)/shard_map/ppermute | solution.py:478
  85.9 1.0 copy-start.1
  95.9 1.2 copy-start.2
  121.5 7.7 %collective-permute-start.4 = (bf16[2,16,640]{2,1,0:T(8,128)(2,1)S(1)}, bf16[2,16,640]{2,1,0:T(8,128)(2,1)S(1)}, u32[]{:S(2)}, u32[]{:S(2)}) collective-permute-start(bf16[2,16,640]{2,1,0:T(8,128)(2,1)S(1)} %get-tuple-element.19), channel_id=1, source_target_pairs={{0,8},{8,16},{16,24},{24,32},{32,40},{40,48},{48,56},{56,64},{64,7... | collective-permute-start | bytes 122888 | tf_op jit(solution)/shard_map/ppermute | solution.py:469
  121.5 7.6 %collective-permute-start.5 = (bf16[2,16,640]{2,1,0:T(8,128)(2,1)S(1)}, bf16[2,16,640]{2,1,0:T(8,128)(2,1)S(1)}, u32[]{:S(2)}, u32[]{:S(2)}) collective-permute-start(bf16[2,16,640]{2,1,0:T(8,128)(2,1)S(1)} %get-tuple-element.20), channel_id=1, source_target_pairs={{0,120},{8,0},{16,8},{24,16},{32,24},{40,32},{48,40},{56,48},{64,5... | collective-permute-start | bytes 122888 | tf_op jit(solution)/shard_map/ppermute | solution.py:469

commit v5 on v4

--- a/solution.py
+++ b/solution.py
@@ -10,7 +10,7 @@
 
 GRID = 4096
 RELAX = 0.15
-VMEM_LIMIT = 28 * 1024 * 1024
+VMEM_LIMIT = 40 * 1024 * 1024
 PAD = 72
 NT = (((1,), (1,)), ((), ()))
 

time: 135 us -> 135 us (level)
  no operation moved by 1% of the time
where the time goes in v5:
time: 135 us; the launch traced here: 134 us
  waiting for transfers between devices  50 us (37%)
  starting transfers between devices  29 us (21%)
  Pallas kernels  28.3 us (21%)
  blocking collectives  21.1 us (16%)
  local copies, waits for them, and re-layouts  4.12 us (3%)
    ppermute x4, waiting for transfers between devices, between_y(): return lax.ppermute(value, ('yh', 'gz'), pairs)  41 us
    all_to_all x1, blocking collectives, exchanged(): return lax.all_to_all(array, axes, split_axis=0, concat_axis=0, tiled=True)  21.1 us
    all_to_all x2, starting transfers between devices, exchanged(): return lax.all_to_all(array, axes, split_axis=0, concat_axis=0, tiled=True)  16.3 us
    pallas_call x3, Pallas kernels, x_transform(): pl.pallas_call(lambda *refs: x_kernel(fields, rows_local, *refs), grid=(r...  14 us
    all_to_all x2, waiting for transfers between devices, exchanged(): return lax.all_to_all(array, axes, split_axis=0, concat_axis=0, tiled=True)  9.01 us
    ppermute x4, starting transfers between devices, between_y(): return lax.ppermute(value, ('yh', 'gz'), pairs)  7.22 us
    ppermute x2, starting transfers between devices, ring(): lax.ppermute(value, axis, [(i, (i + steps) % count) for i in range(count)])  5.42 us
    pallas_call x2, Pallas kernels, y_transform(): pl.pallas_call(kernel, out_shape=jax.ShapeDtypeStruct((8, 32, 2176), jnp....  4.67 us
  transfers between devices with their start and end apart: 8, of which 4 were waited for; matrix products, arithmetic and copies ran while one was open for 0% of the time, Pallas kernels for 11%

profile of v5, /device:TPU:0, one launch (start us, length us, event | category | flops | bytes accessed | tf_op | source)
XLA Modules:
  0.0 133.6 jit_solution(5493922486859253000)
XLA Ops:
  0.0 0.1 fusion.41
  0.1 0.3 fusion.39
  0.5 0.0 copy-start
  0.5 1.9 %copy-done = bf16[3,2,1,64,4096]{4,3,2,1,0:T(8,128)(2,1)S(1)} copy-done((bf16[3,2,1,64,4096]{4,3,2,1,0:T(8,128)(2,1)S(1)}, bf16[3,2,1,64,4096]{4,3,2,1,0:T(8,128)(2,1)}, u32[]{:S(2)}) %copy-start) | copy-done | bytes 3145752
  2.4 5.4 %lines_curl_x_curl_y.1 = (bf16[32,128,128]{2,1,0:T(8,128)(2,1)S(1)}, bf16[32,128,128]{2,1,0:T(8,128)(2,1)}) custom-call(bf16[3,2,64,4096]{3,2,1,0:T(8,128)(2,1)S(1)} %bitcast.1, bf16[3,2,64,4096]{3,2,1,0:T(8,128)(2,1)S(1)} %bitcast.2, bf16[3,2,64,4096]{3,2,1,0:T(8,128)(2,1)S(1)} %bitcast.3, bf16[512,256]{1,0:T(8,128)(2,1)S(1)} %pad_maximum_fusion.refs_3_.refs_2_, ...), custom_call_target="tpu_custom_call" | custom-call | flops 1073741824 | bytes 4194304 | tf_op jit(solution)/shard_map/lines_curl_x_curl_y/pallas_call | solution.py:177
  7.8 3.3 %collective-permute-start = (bf16[32,128,128]{2,1,0:T(8,128)(2,1)}, bf16[32,128,128]{2,1,0:T(8,128)(2,1)S(1)}, u32[]{:S(2)}, u32[]{:S(2)}) collective-permute-start(bf16[32,128,128]{2,1,0:T(8,128)(2,1)} %get-tuple-element.14), channel_id=1, source_target_pairs={{0,64},{1,65},{64,0},{65,1},{2,66},{3,67},{66,2},{67,3},{4,68},{5,... | collective-permute-start | bytes 3145736 | tf_op jit(solution)/shard_map/ppermute | solution.py:478
  11.1 3.5 %lines_curl_z.1.refs_4_ = bf16[32,128,128]{2,1,0:T(8,128)(2,1)} custom-call(bf16[3,2,64,4096]{3,2,1,0:T(8,128)(2,1)S(1)} %bitcast.4, bf16[3,2,64,4096]{3,2,1,0:T(8,128)(2,1)S(1)} %bitcast.5, bf16[512,256]{1,0:T(8,128)(2,1)S(1)} %pad_maximum_fusion.refs_3_.refs_2_, f32[2,32,128]{2,1,0:T(8,128)S(1)} %maximum_multiply_fusion.1.refs_4_.refs_3_, ...), custom_call_target="tpu_custom_call" | custom-call | flops 1073741824 | bytes 4194304 | tf_op jit(solution)/shard_map/lines_curl_z/pallas_call | solution.py:177
  14.5 5.1 %lines_u_v.1 = (bf16[32,128,128]{2,1,0:T(8,128)(2,1)}, bf16[32,128,128]{2,1,0:T(8,128)(2,1)}) custom-call(bf16[3,2,64,4096]{3,2,1,0:T(8,128)(2,1)S(1)} %bitcast.6, bf16[3,2,64,4096]{3,2,1,0:T(8,128)(2,1)S(1)} %bitcast.7, bf16[512,256]{1,0:T(8,128)(2,1)S(1)} %pad_maximum_fusion.refs_3_.refs_2_, f32[2,32,128]{2,1,0:T(8,128)S(1)} %maximum_multiply_fusion.1.refs_4_.refs_3_, ...), custom_call_target="tpu_custom_call" | custom-call | flops 1073741824 | bytes 4194304 | tf_op jit(solution)/shard_map/lines_u_v/pallas_call | solution.py:177
  19.7 0.7 collective-permute-start.1
  20.3 0.4 collective-permute-start.2
  20.7 8.2 %all-to-all-start.1 = ((bf16[32,128,128]{2,1,0:T(8,128)(2,1)}), bf16[32,128,128]{2,1,0:T(8,128)(2,1)S(1)}, u32[]{:S(2)}, u32[]{:S(2)}) async-start(bf16[32,128,128]{2,1,0:T(8,128)(2,1)} %lines_curl_z.1.refs_4_), calls=%async_computation.1 | async-start | bytes 2097152 | tf_op jit(solution)/shard_map/all_to_all | solution.py:486
  28.9 6.7 %collective-permute-done.came = bf16[32,128,128]{2,1,0:T(8,128)(2,1)S(1)} collective-permute-done((bf16[32,128,128]{2,1,0:T(8,128)(2,1)}, bf16[32,128,128]{2,1,0:T(8,128)(2,1)S(1)}, u32[]{:S(2)}, u32[]{:S(2)}) %collective-permute-start) | collective-permute-done | bytes 1048608 | tf_op jit(solution)/shard_map/ppermute | solution.py:478
  35.6 21.9 %collective-permute-done.1.near = bf16[32,128,128]{2,1,0:T(8,128)(2,1)} collective-permute-done((bf16[32,128,128]{2,1,0:T(8,128)(2,1)}, bf16[32,128,128]{2,1,0:T(8,128)(2,1)}, u32[]{:S(2)}, u32[]{:S(2)}) %collective-permute-start.1) | collective-permute-done | bytes 1048608 | tf_op jit(solution)/shard_map/ppermute | solution.py:478
  57.4 2.8 %meet.1 = bf16[32,256,128]{2,1,0:T(8,128)(2,1)} custom-call(bf16[32,128,128]{2,1,0:T(8,128)(2,1)S(1)} %get-tuple-element.13.refs_4_.own, bf16[32,128,128]{2,1,0:T(8,128)(2,1)S(1)} %collective-permute-done.came, bf16[32,128,128]{2,1,0:T(8,128)(2,1)} %collective-permute-done.1.near, bf16[32,128,128]{2,1,0:T(8,128)(2,1)} %collective-permute-done.2.across), custom_call_target="tpu_custom_call" | custom-call | flops 1048576 | bytes 4194304 | tf_op jit(solution)/shard_map/meet/pallas_call | solution.py:205
  60.3 8.2 %all-to-all-start = ((bf16[32,256,128]{2,1,0:T(8,128)(2,1)}), bf16[32,256,128]{2,1,0:T(8,128)(2,1)S(1)}, u32[]{:S(2)}, u32[]{:S(2)}) async-start(bf16[32,256,128]{2,1,0:T(8,128)(2,1)} %meet.1), calls=%async_computation | async-start | bytes 4194304 | tf_op jit(solution)/shard_map/all_to_all | solution.py:486
  68.4 0.1 sine_negate_fusion
  68.6 2.9 %collective-permute-start.3 = (bf16[32,64,128]{2,1,0:T(8,128)(2,1)S(1)}, bf16[32,64,128]{2,1,0:T(8,128)(2,1)S(1)}, u32[]{:S(2)}, u32[]{:S(2)}) collective-permute-start(bf16[32,64,128]{2,1,0:T(8,128)(2,1)S(1)} %slice.4), channel_id=1, source_target_pairs={{0,64},{1,65},{64,0},{65,1},{2,66},{3,67},{66,2},{67,3},{4,68},{5,... | collective-permute-start | bytes 1572872 | tf_op jit(solution)/shard_map/ppermute | solution.py:478
  71.5 0.1 fusion.29
  71.7 0.1 pad_maximum_fusion.2.twist
  71.8 0.1 reduce-precision_convert_fusion.1
  71.9 12.4 %collective-permute-done.3.came = bf16[32,64,128]{2,1,0:T(8,128)(2,1)S(1)} collective-permute-done((bf16[32,64,128]{2,1,0:T(8,128)(2,1)S(1)}, bf16[32,64,128]{2,1,0:T(8,128)(2,1)S(1)}, u32[]{:S(2)}, u32[]{:S(2)}) %collective-permute-start.3) | collective-permute-done | bytes 524320 | tf_op jit(solution)/shard_map/ppermute | solution.py:478
  84.3 1.6 %y_first.1.before = f32[128,2048]{1,0:T(8,128)S(1)} custom-call(bf16[32,128,128]{2,1,0:T(8,128)(2,1)S(1)} %all-to-all-done.1.own, bf16[32,64,128]{2,1,0:T(8,128)(2,1)S(1)} %collective-permute-done.3.came, bf16[256,256]{1,0:T(8,128)(2,1)S(1)} %pad_maximum_fusion.1.matrix, f32[2,64,128]{2,1,0:T(8,128)S(1)} %pad_maximum_fusion.2.twist), custom_call_target="tpu_custom_call" | custom-call | flops 268435456 | bytes 4194304 | tf_op jit(solution)/shard_map/y_first/pallas_call | solution.py:288
  85.9 1.0 copy-done.1
  86.9 9.0 %all-to-all-done.source = bf16[32,256,128]{2,1,0:T(8,128)(2,1)S(1)} async-done(((bf16[32,256,128]{2,1,0:T(8,128)(2,1)}), bf16[32,256,128]{2,1,0:T(8,128)(2,1)S(1)}, u32[]{:S(2)}, u32[]{:S(2)}) %all-to-all-start) | async-done | bytes 2097184 | tf_op jit(solution)/shard_map/all_to_all | solution.py:486
  95.9 1.2 copy-done.2
  97.1 3.1 %y_last.1 = bf16[8,32,2176]{2,1,0:T(8,128)(2,1)S(1)} custom-call(bf16[32,256,128]{2,1,0:T(8,128)(2,1)S(1)} %all-to-all-done.source, f32[128,2048]{1,0:T(8,128)S(1)} %copy-done.2, bf16[256,256]{1,0:T(8,128)(2,1)S(1)} %pad_maximum_fusion.1.matrix, f32[2,64,128]{2,1,0:T(8,128)S(1)} %pad_maximum_fusion.2.twist), custom_call_target="tpu_custom_call" | custom-call | flops 268435456 | bytes 4194304 | tf_op jit(solution)/shard_map/y_last/pallas_call | solution.py:288
  100.2 21.1 %all_to_all.15.field = bf16[8,32,2176]{2,1,0:T(8,128)(2,1)S(1)} all-to-all(bf16[8,32,2176]{2,1,0:T(8,128)(2,1)S(1)} %y_last.1), channel_id=1, replica_groups=mesh['yh'=2,'zc'=8,'col'=4,'gz'=2] {'gz','col'}, dimensions={0} | all-to-all | bytes 2228224 | tf_op jit(solution)/shard_map/all_to_all | solution.py:486
  121.3 0.1 edges.1
  121.5 0.1 collective-permute-start.4
  121.5 5.3 %collective-permute-start.5 = (bf16[2,16,640]{2,1,0:T(8,128)(2,1)S(1)}, bf16[2,16,640]{2,1,0:T(8,128)(2,1)S(1)}, u32[]{:S(2)}, u32[]{:S(2)}) collective-permute-start(bf16[2,16,640]{2,1,0:T(8,128)(2,1)S(1)} %get-tuple-element.20), channel_id=1, source_target_pairs={{0,120},{8,0},{16,8},{24,16},{32,24},{40,32},{48,40},{56,48},{64,5... | collective-permute-start | bytes 122888 | tf_op jit(solution)/shard_map/ppermute | solution.py:469
  126.9 2.2 %regroup.1 = (f32[72,16,256]{2,1,0:T(8,128)S(1)}, f32[72,16,256]{2,1,0:T(8,128)S(1)}) custom-call(bf16[8,32,2176]{2,1,0:T(8,128)(2,1)S(1)} %all_to_all.15.field), custom_call_target="tpu_custom_call" | custom-call | flops 16777216 | bytes 8388608 | tf_op jit(solution)/shard_map/regroup/pallas_call | solution.py:358
  129.1 4.5 %smooth.1 = f32[1,1024,256]{2,1,0:T(8,128)} custom-call(f32[72,16,256]{2,1,0:T(8,128)S(1)} %get-tuple-element.17.own, f32[72,16,256]{2,1,0:T(8,128)S(1)} %get-tuple-element.18.other, bf16[2,16,640]{2,1,0:T(8,128)(2,1)S(1)} %collective-permute-done.4.low, bf16[2,16,640]{2,1,0:T(8,128)(2,1)S(1)} %collective-permute-done.5.high), custom_call_target="tpu_custom_call" | custom-call | tf_op jit(solution)/shard_map/smooth/pallas_call | solution.py:453
  (15 shorter events, 0.1 us)
Async XLA Ops:
  0.5 1.9 %copy-start = (bf16[3,2,1,64,4096]{4,3,2,1,0:T(8,128)(2,1)S(1)}, bf16[3,2,1,64,4096]{4,3,2,1,0:T(8,128)(2,1)}, u32[]{:S(2)}) copy-start(bf16[3,2,1,64,4096]{4,3,2,1,0:T(8,128)(2,1)} %param.1) | copy-start | bytes 9437188
  7.8 27.8 %collective-permute-start = (bf16[32,128,128]{2,1,0:T(8,128)(2,1)}, bf16[32,128,128]{2,1,0:T(8,128)(2,1)S(1)}, u32[]{:S(2)}, u32[]{:S(2)}) collective-permute-start(bf16[32,128,128]{2,1,0:T(8,128)(2,1)} %get-tuple-element.14), channel_id=1, source_target_pairs={{0,64},{1,65},{64,0},{65,1},{2,66},{3,67},{66,2},{67,3},{4,68},{5,... | collective-permute-start | bytes 3145736 | tf_op jit(solution)/shard_map/ppermute | solution.py:478
  19.7 37.8 %collective-permute-start.1 = (bf16[32,128,128]{2,1,0:T(8,128)(2,1)}, bf16[32,128,128]{2,1,0:T(8,128)(2,1)}, u32[]{:S(2)}, u32[]{:S(2)}) collective-permute-start(bf16[32,128,128]{2,1,0:T(8,128)(2,1)} %get-tuple-element.15), channel_id=1, source_target_pairs={{0,1},{1,0},{64,65},{65,64},{2,3},{3,2},{66,67},{67,66},{4,5},{5,4... | collective-permute-start | bytes 3145736 | tf_op jit(solution)/shard_map/ppermute | solution.py:478
  20.3 37.1 %collective-permute-start.2 = (bf16[32,128,128]{2,1,0:T(8,128)(2,1)}, bf16[32,128,128]{2,1,0:T(8,128)(2,1)}, u32[]{:S(2)}, u32[]{:S(2)}) collective-permute-start(bf16[32,128,128]{2,1,0:T(8,128)(2,1)} %get-tuple-element.16), channel_id=1, source_target_pairs={{0,65},{1,64},{64,1},{65,0},{2,67},{3,66},{66,3},{67,2},{4,69},{5,... | collective-permute-start | bytes 3145736 | tf_op jit(solution)/shard_map/ppermute | solution.py:478
  20.7 39.5 %all-to-all-start.1 = ((bf16[32,128,128]{2,1,0:T(8,128)(2,1)}), bf16[32,128,128]{2,1,0:T(8,128)(2,1)S(1)}, u32[]{:S(2)}, u32[]{:S(2)}) async-start(bf16[32,128,128]{2,1,0:T(8,128)(2,1)} %lines_curl_z.1.refs_4_), calls=%async_computation.1 | async-start | bytes 2097152 | tf_op jit(solution)/shard_map/all_to_all | solution.py:486
  60.3 35.6 %all-to-all-start = ((bf16[32,256,128]{2,1,0:T(8,128)(2,1)}), bf16[32,256,128]{2,1,0:T(8,128)(2,1)S(1)}, u32[]{:S(2)}, u32[]{:S(2)}) async-start(bf16[32,256,128]{2,1,0:T(8,128)(2,1)} %meet.1), calls=%async_computation | async-start | bytes 4194304 | tf_op jit(solution)/shard_map/all_to_all | solution.py:486
  68.6 15.7 %collective-permute-start.3 = (bf16[32,64,128]{2,1,0:T(8,128)(2,1)S(1)}, bf16[32,64,128]{2,1,0:T(8,128)(2,1)S(1)}, u32[]{:S(2)}, u32[]{:S(2)}) collective-permute-start(bf16[32,64,128]{2,1,0:T(8,128)(2,1)S(1)} %slice.4), channel_id=1, source_target_pairs={{0,64},{1,65},{64,0},{65,1},{2,66},{3,67},{66,2},{67,3},{4,68},{5,... | collective-permute-start | bytes 1572872 | tf_op jit(solution)/shard_map/ppermute | solution.py:478
  85.9 1.0 copy-start.1
  95.9 1.2 copy-start.2
  121.5 7.7 %collective-permute-start.4 = (bf16[2,16,640]{2,1,0:T(8,128)(2,1)S(1)}, bf16[2,16,640]{2,1,0:T(8,128)(2,1)S(1)}, u32[]{:S(2)}, u32[]{:S(2)}) collective-permute-start(bf16[2,16,640]{2,1,0:T(8,128)(2,1)S(1)} %get-tuple-element.19), channel_id=1, source_target_pairs={{0,8},{8,16},{16,24},{24,32},{32,40},{40,48},{48,56},{56,64},{64,7... | collective-permute-start | bytes 122888 | tf_op jit(solution)/shard_map/ppermute | solution.py:469
  121.5 7.6 %collective-permute-start.5 = (bf16[2,16,640]{2,1,0:T(8,128)(2,1)S(1)}, bf16[2,16,640]{2,1,0:T(8,128)(2,1)S(1)}, u32[]{:S(2)}, u32[]{:S(2)}) collective-permute-start(bf16[2,16,640]{2,1,0:T(8,128)(2,1)S(1)} %get-tuple-element.20), channel_id=1, source_target_pairs={{0,120},{8,0},{16,8},{24,16},{32,24},{40,32},{48,40},{56,48},{64,5... | collective-permute-start | bytes 122888 | tf_op jit(solution)/shard_map/ppermute | solution.py:469
